TPU v7x, 32 devices: a whole 2x2x4 slice. The times are simulated.
32 devices in a mesh: groups: 2 (over y), col: 4 (over x, core), row: 4 (over z).
Axes of the slice: x: 2, y: 2, z: 4, core: 2. Of those that a mesh axis runs over, the one named last changes fastest.
Arguments:
- object_field: float32 [2, 3072, 1536], P(None, ('groups', 'row'), 'col'), parts along dimension 1, may hold values from -7 to 7
- probe: float32 [2, 4, 256, 256], P(None, 'groups'), parts along dimension 1, may hold values from -2 to 2
- positions: int32 [8, 4, 2, 8], P(('groups', 'row'), 'col'), parts along dimension 0, may hold values from 0 to 383
- counts: int32 [8, 4], P(('groups', 'row'), 'col'), parts along dimension 0, may hold values from 1 to 8, as said below
- patterns: bfloat16 [8, 4, 8, 256, 256], P(('groups', 'row'), 'col'), parts along dimension 0, may hold values from 0 to 1
Outputs:
- object_grad: float32 [2, 3072, 1536], P(None, ('groups', 'row'), 'col'), parts along dimension 1
- probe_grad: float32 [2, 4, 256, 256], P(None, 'groups'), parts along dimension 1
There are 2 independent parts, one for each index of `groups`. A program takes and returns all parts, laid end to end along the dimension named above; each array names one. Nothing has to cross between parts.
Inputs may be any that keep to these rules, and one draw needn't show every extreme that they name: `counts`: at least one tile holds 8 live positions in every draw.
All inputs are finite; a program needn't handle non-finite values.
Results may differ from a plain program's by a relative error of at most 0.005.
Values sent between devices are 32-bit elements; how exact they have to be, the bound alone decides.
No kernel may reach another device: no remote copies, remote signals or barrier semaphores. Data moves between devices by JAX's collectives and lax.ppermute only.
A program may use at most 64 MiB of HBM per device.

v0:
```python
import math

import jax
import jax.numpy as jnp
from jax import lax
from jax.sharding import PartitionSpec as P

W = 256
MODES = 2
KMAX = 8


def extended_2(x, sides, width):
    for axis, dim in sides:
        size, length = (lax.axis_size(axis), x.shape[dim])
        up = [(i, (i + 1) % size) for i in range(size - 1)]
        down = [(j, i) for i, j in up]
        last = lax.slice_in_dim(x, length - width, length, axis=dim)
        initial = lax.slice_in_dim(x, 0, width, axis=dim)
        before = lax.ppermute(last, axis, up)
        after = lax.ppermute(initial, axis, down)
        x = jnp.concatenate([before, x, after], axis=dim)
    return x


def dft_tables():
    counter = jnp.arange(W, dtype=jnp.int32)
    phases = counter[:, None] * counter[None, :] % W
    angles = 2.0 * math.pi / W * phases.astype(jnp.float32)
    scaling = 1.0 / math.sqrt(W)
    return (
        (jnp.cos(angles) * scaling).astype(jnp.bfloat16),
        (jnp.sin(angles) * scaling).astype(jnp.bfloat16),
    )


def right_factor(cosine_table, sine_table, direction):
    upper = jnp.concatenate([cosine_table, -direction * sine_table], axis=1)
    lower = jnp.concatenate([direction * sine_table, cosine_table], axis=1)
    return jnp.concatenate([upper, lower], axis=0)


def transform(wavefield, cosine_table, sine_table, direction):
    factor = right_factor(cosine_table, sine_table, direction)
    halfway = jnp.einsum(
        "bjx,xy->bjy", wavefield, factor, preferred_element_type=jnp.float32
    ).astype(jnp.bfloat16)
    with_cosine = jnp.einsum(
        "jk,bkx->bjx", cosine_table, halfway, preferred_element_type=jnp.float32
    )
    with_sine = jnp.einsum("jk,bkx->bjx", sine_table, halfway, preferred_element_type=jnp.float32)
    real_part = with_cosine[..., :W] + direction * with_sine[..., W:]
    imag_part = with_cosine[..., W:] - direction * with_sine[..., :W]
    return (real_part, imag_part)


def local(object_field, probe, positions, counts, patterns):
    margin = W // 2
    padded = extended_2(object_field, (("col", 2), ("row", 1)), margin)
    cosine_table, sine_table = dft_tables()
    offsets = positions[0, 0]
    live_count = counts[0, 0]
    measured_all = patterns[0, 0]
    probe_real = probe[0][None]
    probe_imag = probe[1][None]
    per_block = 2

    def one_block(block_index, carry):
        gradient, probe_total = carry
        first_slot = block_index * per_block
        corners = [
            (0, offsets[0, first_slot + slot_index], offsets[1, first_slot + slot_index])
            for slot_index in range(per_block)
        ]
        patches = jnp.stack([lax.dynamic_slice(padded, corner, (2, W, W)) for corner in corners])
        object_real = patches[:, 0][:, None]
        object_imag = patches[:, 1][:, None]
        wave_real = probe_real * object_real - probe_imag * object_imag
        wave_imag = probe_real * object_imag + probe_imag * object_real
        wavefield = (
            jnp.concatenate([wave_real, wave_imag], axis=-1)
            .reshape(per_block * MODES, W, 2 * W)
            .astype(jnp.bfloat16)
        )
        far_real, far_imag = transform(wavefield, cosine_table, sine_table, 1.0)
        far_real = far_real.reshape(per_block, MODES, W, W)
        far_imag = far_imag.reshape(per_block, MODES, W, W)
        intensity = jnp.sum(far_real * far_real + far_imag * far_imag, axis=1)
        measured = lax.dynamic_slice_in_dim(measured_all, first_slot, per_block, 0).astype(
            jnp.float32
        )
        live_mask = (first_slot + jnp.arange(per_block, dtype=jnp.int32) < live_count).astype(
            jnp.float32
        )
        residual = live_mask[:, None, None] * (intensity - measured)
        weighted = jnp.concatenate(
            [residual[:, None] * far_real, residual[:, None] * far_imag], axis=-1
        )
        weighted = weighted.reshape(per_block * MODES, W, 2 * W).astype(jnp.bfloat16)
        back_real, back_imag = transform(weighted, cosine_table, sine_table, -1.0)
        back_real = back_real.reshape(per_block, MODES, W, W)
        back_imag = back_imag.reshape(per_block, MODES, W, W)
        object_terms = jnp.stack(
            [
                jnp.sum(probe_real * back_real + probe_imag * back_imag, axis=1),
                jnp.sum(probe_real * back_imag - probe_imag * back_real, axis=1),
            ],
            axis=1,
        )
        probe_terms = jnp.stack(
            [
                jnp.sum(object_real * back_real + object_imag * back_imag, axis=0),
                jnp.sum(object_real * back_imag - object_imag * back_real, axis=0),
            ]
        )
        for slot_index in range(per_block):
            current = lax.dynamic_slice(gradient, corners[slot_index], (2, W, W))
            gradient = lax.dynamic_update_slice(
                gradient, current + object_terms[slot_index], corners[slot_index]
            )
        return (gradient, probe_total + probe_terms)

    block_count = KMAX // per_block
    start = (jnp.zeros(padded.shape, jnp.float32), jnp.zeros(probe.shape, jnp.float32))
    gradient, probe_total = lax.fori_loop(0, block_count, one_block, start)
    tile_size = object_field.shape[1]
    extended = extended_2(gradient, (("col", 2), ("row", 1)), margin)
    far_edge = tile_size + 3 * margin
    middle = slice(2 * margin, 2 * margin + tile_size)
    interior = gradient[:, margin : margin + tile_size, margin : margin + tile_size]
    interior = interior.at[:, :margin, :].add(extended[:, :margin, middle])
    interior = interior.at[:, tile_size - margin :, :].add(extended[:, far_edge:, middle])
    interior = interior.at[:, :, :margin].add(extended[:, middle, :margin])
    interior = interior.at[:, :, tile_size - margin :].add(extended[:, middle, far_edge:])
    interior = interior.at[:, :margin, :margin].add(extended[:, :margin, :margin])
    interior = interior.at[:, :margin, tile_size - margin :].add(extended[:, :margin, far_edge:])
    interior = interior.at[:, tile_size - margin :, :margin].add(extended[:, far_edge:, :margin])
    interior = interior.at[:, tile_size - margin :, tile_size - margin :].add(
        extended[:, far_edge:, far_edge:]
    )
    count_here = live_count.astype(jnp.float32)
    summed_terms, summed_count = lax.psum((probe_total, count_here), ("col", "row"))
    return (interior, summed_terms / summed_count)


def solution(mesh):
    placed = (
        P(None, ("groups", "row"), "col"),
        P(None, "groups", None, None),
        P(("groups", "row"), "col", None, None),
        P(("groups", "row"), "col"),
        P(("groups", "row"), "col", None, None, None),
    )
    return jax.shard_map(
        local,
        mesh=mesh,
        in_specs=placed,
        out_specs=(P(None, ("groups", "row"), "col"), P(None, "groups", None, None)),
        check_vma=False,
    )
```

profile of v0, /device:TPU:5, one launch (start us, length us, event | category | flops | bytes accessed | tf_op | source)
XLA Modules:
  0.0 381.2 jit_solution(16355979385493019969)
XLA Ops:
  8.5 3.7 collective-permute-start
  12.2 1.9 collective-permute-start.1
  14.1 2.8 collective-permute-done
  17.0 4.3 %collective-permute-done.1 = f32[2,384,128]{2,1,0:T(8,128)S(1)} collective-permute-done((f32[2,384,128]{2,1,0:T(8,128)S(1)}, f32[2,384,128]{2,1,0:T(8,128)S(1)}, u32[]{:S(2)}, u32[]{:S(2)}) %collective-permute-start.1) | collective-permute-done | bytes 393248 | tf_op jit(solution)/shard_map/ppermute | solution.py:21
  22.5 4.0 %collective-permute-start.2 = (f32[2,128,640]{2,1,0:T(8,128)}, f32[2,128,640]{2,1,0:T(8,128)}, u32[]{:S(2)}, u32[]{:S(2)}) collective-permute-start(f32[2,128,640]{2,1,0:T(8,128)} %get-tuple-element.518), channel_id=1, source_target_pairs={{0,1},{1,2},{2,3},{4,5},{5,6},{6,7},{8,9},{9,10},{10,11},{12,13},{... | collective-permute-start | bytes 1966088 | tf_op jit(solution)/shard_map/ppermute | solution.py:20
  31.0 2.4 fusion.80
  33.4 2.2 collective-permute-done.2
  35.5 4.9 %collective-permute-done.3 = f32[2,128,640]{2,1,0:T(8,128)} collective-permute-done((f32[2,128,640]{2,1,0:T(8,128)}, f32[2,128,640]{2,1,0:T(8,128)}, u32[]{:S(2)}, u32[]{:S(2)}) %collective-permute-start.3) | collective-permute-done | bytes 655392 | tf_op jit(solution)/shard_map/ppermute | solution.py:21
  40.5 3.2 pad_maximum_fusion.2
  43.6 1.9 broadcast_in_dim.15
  45.6 199.2 %while.27 = (s32[]{:T(128)}, f32[2,640,640]{2,1,0:T(8,128)}, f32[2,2,256,256]{3,2,1,0:T(8,128)}, s32[2,8]{1,0:T(2,128)S(1)}, f32[1,2,256,256]{3,2,1,0:T(8,128)},...) while((s32[]{:T(128)}, f32[2,640,640]{2,1,0:T(8,128)}, ...), condition=%wide.region_6.7_spmd.clone.clone, body=%wide.region_0.6_spmd.clone.clone.sunk | while | flops 2174222336 | bytes 63439348 | solution.py:125
  53.7 1.8 dynamic-slice_bitcast_fusion.3
  59.0 1.7 convolution_convert_fusion.4
  70.9 1.6 copy.28
  73.7 3.4 add_reduce_fusion.3
  77.1 2.3 maximum_add_fusion.2
  80.8 6.3 %dynamic_update_slice.26 = f32[2,640,640]{2,1,0:T(8,128)} dynamic-update-slice(f32[2,640,640]{2,1,0:T(8,128)} %get-tuple-element.651, f32[2,256,256]{2,1,0:T(8,128)S(1)} %fusion.116, s32[]{:T(128)} %constant.316.clone.1..sunk, s32[]{:T(128)S(6)} %select_n.173, s32[]{:T(128)S(6)} %select_n.174) | dynamic-update-slice | bytes 1048580 | tf_op jit(solution)/shard_map/while/body/eval_jaxpr/dynamic_update_slice | solution.py:118
  88.4 6.5 %dynamic_update_slice.27 = f32[2,640,640]{2,1,0:T(8,128)} dynamic-update-slice(f32[2,640,640]{2,1,0:T(8,128)} %dynamic_update_slice.26, f32[2,256,256]{2,1,0:T(8,128)S(1)} %fusion.117, s32[]{:T(128)} %constant.316.clone.1..sunk, s32[]{:T(128)S(6)} %select_n.175, s32[]{:T(128)S(6)} %select_n.176) | dynamic-update-slice | bytes 1048580 | tf_op jit(solution)/shard_map/while/body/eval_jaxpr/dynamic_update_slice | solution.py:118
  103.0 1.8 dynamic-slice_bitcast_fusion.3
  108.4 1.7 convolution_convert_fusion.4
  123.1 3.4 add_reduce_fusion.3
  126.5 2.7 maximum_add_fusion.2
  130.5 6.6 %dynamic_update_slice.26 = f32[2,640,640]{2,1,0:T(8,128)} dynamic-update-slice(f32[2,640,640]{2,1,0:T(8,128)} %get-tuple-element.651, f32[2,256,256]{2,1,0:T(8,128)S(1)} %fusion.116, s32[]{:T(128)} %constant.316.clone.1..sunk, s32[]{:T(128)S(6)} %select_n.173, s32[]{:T(128)S(6)} %select_n.174) | dynamic-update-slice | bytes 1048580 | tf_op jit(solution)/shard_map/while/body/eval_jaxpr/dynamic_update_slice | solution.py:118
  138.4 6.5 %dynamic_update_slice.27 = f32[2,640,640]{2,1,0:T(8,128)} dynamic-update-slice(f32[2,640,640]{2,1,0:T(8,128)} %dynamic_update_slice.26, f32[2,256,256]{2,1,0:T(8,128)S(1)} %fusion.117, s32[]{:T(128)} %constant.316.clone.1..sunk, s32[]{:T(128)S(6)} %select_n.175, s32[]{:T(128)S(6)} %select_n.176) | dynamic-update-slice | bytes 1048580 | tf_op jit(solution)/shard_map/while/body/eval_jaxpr/dynamic_update_slice | solution.py:118
  153.1 1.8 dynamic-slice_bitcast_fusion.3
  158.4 1.7 convolution_convert_fusion.4
  173.1 3.4 add_reduce_fusion.3
  176.5 2.7 maximum_add_fusion.2
  180.5 6.8 %dynamic_update_slice.26 = f32[2,640,640]{2,1,0:T(8,128)} dynamic-update-slice(f32[2,640,640]{2,1,0:T(8,128)} %get-tuple-element.651, f32[2,256,256]{2,1,0:T(8,128)S(1)} %fusion.116, s32[]{:T(128)} %constant.316.clone.1..sunk, s32[]{:T(128)S(6)} %select_n.173, s32[]{:T(128)S(6)} %select_n.174) | dynamic-update-slice | bytes 1048580 | tf_op jit(solution)/shard_map/while/body/eval_jaxpr/dynamic_update_slice | solution.py:118
  188.6 6.1 %dynamic_update_slice.27 = f32[2,640,640]{2,1,0:T(8,128)} dynamic-update-slice(f32[2,640,640]{2,1,0:T(8,128)} %dynamic_update_slice.26, f32[2,256,256]{2,1,0:T(8,128)S(1)} %fusion.117, s32[]{:T(128)} %constant.316.clone.1..sunk, s32[]{:T(128)S(6)} %select_n.175, s32[]{:T(128)S(6)} %select_n.176) | dynamic-update-slice | bytes 1048580 | tf_op jit(solution)/shard_map/while/body/eval_jaxpr/dynamic_update_slice | solution.py:118
  202.8 1.8 dynamic-slice_bitcast_fusion.3
  208.2 1.7 convolution_convert_fusion.4
  222.9 3.4 add_reduce_fusion.3
  226.3 2.7 maximum_add_fusion.2
  230.3 6.5 %dynamic_update_slice.26 = f32[2,640,640]{2,1,0:T(8,128)} dynamic-update-slice(f32[2,640,640]{2,1,0:T(8,128)} %get-tuple-element.651, f32[2,256,256]{2,1,0:T(8,128)S(1)} %fusion.116, s32[]{:T(128)} %constant.316.clone.1..sunk, s32[]{:T(128)S(6)} %select_n.173, s32[]{:T(128)S(6)} %select_n.174) | dynamic-update-slice | bytes 1048580 | tf_op jit(solution)/shard_map/while/body/eval_jaxpr/dynamic_update_slice | solution.py:118
  238.2 6.6 %dynamic_update_slice.27 = f32[2,640,640]{2,1,0:T(8,128)} dynamic-update-slice(f32[2,640,640]{2,1,0:T(8,128)} %dynamic_update_slice.26, f32[2,256,256]{2,1,0:T(8,128)S(1)} %fusion.117, s32[]{:T(128)} %constant.316.clone.1..sunk, s32[]{:T(128)S(6)} %select_n.175, s32[]{:T(128)S(6)} %select_n.176) | dynamic-update-slice | bytes 1048580 | tf_op jit(solution)/shard_map/while/body/eval_jaxpr/dynamic_update_slice | solution.py:118
  246.3 2.7 collective-permute-start.4
  249.0 1.9 collective-permute-start.5
  250.9 5.6 %collective-permute-done.4 = f32[2,640,128]{2,1,0:T(8,128)S(1)} collective-permute-done((f32[2,640,128]{2,1,0:T(8,128)S(1)}, f32[2,640,128]{2,1,0:T(8,128)S(1)}, u32[]{:S(2)}, u32[]{:S(2)}) %collective-permute-start.4) | collective-permute-done | bytes 655392 | tf_op jit(solution)/shard_map/ppermute | solution.py:20
  257.6 3.3 collective-permute-done.5
  262.4 3.5 collective-permute-start.6
  267.8 42.6 %psum.15 = f32[]{:T(128)} all-reduce(f32[]{:T(128)S(6)} %convert_element_type.117), channel_id=1, replica_groups=mesh['groups'=2,'col'=4,'row'=4] {'col','row'}, use_global_device_ids=true, to_apply=%region_9.10 | all-reduce | flops 1 | bytes 8 | tf_op jit(solution)/shard_map/psum | solution.py:142
  312.9 43.9 %all-reduce.2.cloned.1.call-done = f32[2,2,256,256]{3,2,1,0:T(8,128)} async-done(((f32[2,2,256,256]{3,2,1,0:T(8,128)}), f32[2,2,256,256]{3,2,1,0:T(8,128)}) %all-reduce.2.cloned.1.call-update) | async-done | bytes 1048592 | tf_op jit(solution)/shard_map/psum | solution.py:142
  356.8 3.1 broadcast_divide_fusion
  364.2 2.9 add_select_fusion.2
  367.1 3.9 %scatter-add.35 = f32[2,384,384]{2,1,0:T(8,128)} dynamic-update-slice(f32[2,384,384]{2,1,0:T(8,128)} %copy-done.2, f32[2,128,128]{2,1,0:T(8,128)S(1)} %add_select_fusion.2, s32[]{:T(128)} %constant.316.clone.1, s32[]{:T(128)} %bitcast.3, s32[]{:T(128)} %bitcast.4) | dynamic-update-slice | bytes 262148 | tf_op jit(solution)/shard_map/scatter-add | solution.py:136
  371.1 1.6 fusion.74
  372.7 1.6 fusion.73
  (126 shorter events, 97.2 us)
Async XLA Ops:
  7.2 9.7 %copy-start.3 = (f32[2,384,384]{2,1,0:T(8,128)S(1)}, f32[2,384,384]{2,1,0:T(8,128)}, u32[]{:S(2)}) copy-start(f32[2,384,384]{2,1,0:T(8,128)} %param.23) | copy-start | bytes 3538948
  7.2 349.6 %all-reduce.2.cloned.1.call-start = ((), (), s32[]{:S(2)}) async-start(), calls=%async_computation | async-start | bytes 2097152 | tf_op jit(solution)/shard_map/psum | solution.py:142
  8.5 8.4 %collective-permute-start = (f32[2,384,128]{2,1,0:T(8,128)S(1)}, f32[2,384,128]{2,1,0:T(8,128)S(1)}, u32[]{:S(2)}, u32[]{:S(2)}) collective-permute-start(f32[2,384,128]{2,1,0:T(8,128)S(1)} %get-tuple-element.521), channel_id=1, source_target_pairs={{0,4},{4,8},{8,12},{1,5},{5,9},{9,13},{2,6},{6,10},{10,14},{3,7},{... | collective-permute-start | bytes 1179656 | tf_op jit(solution)/shard_map/ppermute | solution.py:20
  12.2 9.1 %collective-permute-start.1 = (f32[2,384,128]{2,1,0:T(8,128)S(1)}, f32[2,384,128]{2,1,0:T(8,128)S(1)}, u32[]{:S(2)}, u32[]{:S(2)}) collective-permute-start(f32[2,384,128]{2,1,0:T(8,128)S(1)} %get-tuple-element.520), channel_id=1, source_target_pairs={{4,0},{8,4},{12,8},{5,1},{9,5},{13,9},{6,2},{10,6},{14,10},{7,3},{... | collective-permute-start | bytes 1179656 | tf_op jit(solution)/shard_map/ppermute | solution.py:21
  17.0 10.8 %copy-start.8 = (bf16[1,1,8,256,256]{4,3,2,1,0:T(8,128)(2,1)S(1)}, bf16[1,1,8,256,256]{4,3,2,1,0:T(8,128)(2,1)}, u32[]{:S(2)}) copy-start(bf16[1,1,8,256,256]{4,3,2,1,0:T(8,128)(2,1)} %param.27) | copy-start | bytes 3145732
  22.5 13.0 %collective-permute-start.2 = (f32[2,128,640]{2,1,0:T(8,128)}, f32[2,128,640]{2,1,0:T(8,128)}, u32[]{:S(2)}, u32[]{:S(2)}) collective-permute-start(f32[2,128,640]{2,1,0:T(8,128)} %get-tuple-element.518), channel_id=1, source_target_pairs={{0,1},{1,2},{2,3},{4,5},{5,6},{6,7},{8,9},{9,10},{10,11},{12,13},{... | collective-permute-start | bytes 1966088 | tf_op jit(solution)/shard_map/ppermute | solution.py:20
  26.5 13.9 %collective-permute-start.3 = (f32[2,128,640]{2,1,0:T(8,128)}, f32[2,128,640]{2,1,0:T(8,128)}, u32[]{:S(2)}, u32[]{:S(2)}) collective-permute-start(f32[2,128,640]{2,1,0:T(8,128)} %get-tuple-element.519), channel_id=1, source_target_pairs={{1,0},{2,1},{3,2},{5,4},{6,5},{7,6},{9,8},{10,9},{11,10},{13,12},{... | collective-permute-start | bytes 1966088 | tf_op jit(solution)/shard_map/ppermute | solution.py:21
  43.6 1.9 copy-start.9
  244.7 12.7 %copy-start = (f32[2,640,640]{2,1,0:T(8,128)S(1)}, f32[2,640,640]{2,1,0:T(8,128)}, u32[]{:S(2)}) copy-start(f32[2,640,640]{2,1,0:T(8,128)} %get-tuple-element.393) | copy-start | bytes 9830404
  246.3 10.2 %collective-permute-start.4 = (f32[2,640,128]{2,1,0:T(8,128)S(1)}, f32[2,640,128]{2,1,0:T(8,128)S(1)}, u32[]{:S(2)}, u32[]{:S(2)}) collective-permute-start(f32[2,640,128]{2,1,0:T(8,128)S(1)} %get-tuple-element.517), channel_id=1, source_target_pairs={{0,4},{4,8},{8,12},{1,5},{5,9},{9,13},{2,6},{6,10},{10,14},{3,7},{... | collective-permute-start | bytes 1966088 | tf_op jit(solution)/shard_map/ppermute | solution.py:20
  249.0 11.9 %collective-permute-start.5 = (f32[2,640,128]{2,1,0:T(8,128)S(1)}, f32[2,640,128]{2,1,0:T(8,128)S(1)}, u32[]{:S(2)}, u32[]{:S(2)}) collective-permute-start(f32[2,640,128]{2,1,0:T(8,128)S(1)} %get-tuple-element.516), channel_id=1, source_target_pairs={{4,0},{8,4},{12,8},{5,1},{9,5},{13,9},{6,2},{10,6},{14,10},{7,3},{... | collective-permute-start | bytes 1966088 | tf_op jit(solution)/shard_map/ppermute | solution.py:21
  256.5 0.8 copy-start.4
  260.9 1.5 copy-start.6
  260.9 50.1 %copy-start.10 = (s32[3]{0:T(128)S(1)}, s32[3]{0:T(128)}, u32[]{:S(2)}) copy-start(s32[3]{0:T(128)} %constant.323.clone.1) | copy-start | bytes 40
  262.4 97.5 %collective-permute-start.6 = (f32[2,128,896]{2,1,0:T(8,128)}, f32[2,128,896]{2,1,0:T(8,128)}, u32[]{:S(2)}, u32[]{:S(2)}) collective-permute-start(f32[2,128,896]{2,1,0:T(8,128)} %get-tuple-element.515), channel_id=1, source_target_pairs={{0,1},{1,2},{2,3},{4,5},{5,6},{6,7},{8,9},{9,10},{10,11},{12,13},{... | collective-permute-start | bytes 2752520 | tf_op jit(solution)/shard_map/ppermute | solution.py:20
  265.9 95.1 %collective-permute-start.7 = (f32[2,128,896]{2,1,0:T(8,128)}, f32[2,128,896]{2,1,0:T(8,128)}, u32[]{:S(2)}, u32[]{:S(2)}) collective-permute-start(f32[2,128,896]{2,1,0:T(8,128)} %get-tuple-element.514), channel_id=1, source_target_pairs={{1,0},{2,1},{3,2},{5,4},{6,5},{7,6},{9,8},{10,9},{11,10},{13,12},{... | collective-permute-start | bytes 2752520 | tf_op jit(solution)/shard_map/ppermute | solution.py:21
  356.8 3.1 copy-start.1
  356.8 5.3 %copy-start.5 = (f32[2,640,128]{2,1,0:T(8,128)S(1)}, f32[2,640,128]{2,1,0:T(8,128)}, u32[]{:S(2)}) copy-start(f32[2,640,128]{2,1,0:T(8,128)} %copy-done.4) | copy-start | bytes 1966084
  359.9 2.3 copy-start.7
  363.2 1.0 copy-start.2
Sparse Core Ops, SparseCore 0:
  266.0 90.7 all-reduce.1
where the time goes:
time: 387 us; the launch traced here: 381 us
  local copies, waits for them, and re-layouts  91.9 us (24%)
  other arithmetic  82.2 us (21%)
  waiting for transfers between devices  66.9 us (17%)
  blocking collectives  42.6 us (11%)
  matrix products  32 us (8%)
  loops' own time  30.3 us (8%)
  starting transfers between devices  20.4 us (5%)
  between operations  14.9 us (4%)
    dynamic_update_slice x8, local copies, waits for them, and re-layouts, one_block(): lax.dynamic_update_slice(gradient, current + object_terms[slot_index], co...  51.9 us
    psum x1, waiting for transfers between devices, local(): lax.psum((probe_total, count_here), ('col', 'row'))  43.9 us
    psum x1, blocking collectives, local(): lax.psum((probe_total, count_here), ('col', 'row'))  42.6 us
    another operation x1, loops' own time, local(): gradient, probe_total = lax.fori_loop(0, block_count, one_block, start)  30.3 us
    ppermute x4, starting transfers between devices, extended_2(): before = lax.ppermute(last, axis, up)  13.9 us
    reduce_sum x4, other arithmetic, one_block(): jnp.sum(object_real * back_real + object_imag * back_imag, axis=0)  13.5 us
    ppermute x4, waiting for transfers between devices, extended_2(): after = lax.ppermute(initial, axis, down)  12.5 us
    another operation x11, other arithmetic  11.4 us
  transfers between devices with their start and end apart: 9, of which 7 were waited for; matrix products, arithmetic and copies ran while one was open for 3% of the time, Pallas kernels for 0%

commit v1 on v0

v1 whole, which is shorter than its diff:
```python
import math

import jax
import jax.numpy as jnp
import ml_dtypes
import numpy as np
from jax import lax
from jax.experimental import pallas as pl
from jax.experimental.pallas import tpu as pltpu
from jax.sharding import PartitionSpec as P

W = 256
MODES = 2
KMAX = 8
HALF = W // 2
LANES = 128


def tables():
    counter = np.arange(W)
    phases = (counter[:, None] * counter[None, :] % W).astype(np.float32)
    angles = (np.float32(2.0 * math.pi / W) * phases).astype(np.float32)
    scaling = np.float32(1.0 / math.sqrt(W))
    cosine = (np.cos(angles) * scaling).astype(ml_dtypes.bfloat16)
    sine = (np.sin(angles) * scaling).astype(ml_dtypes.bfloat16)
    ahead = np.block([[cosine, -sine], [sine, cosine]])
    back = np.block([[cosine, sine], [-sine, cosine]])
    return ahead, back


def swap(x, axis, parity):
    size = lax.axis_size(axis)
    pairs = [(i, i + 1) for i in range(parity, size - 1, 2)]
    return lax.ppermute(x, axis, pairs + [(j, i) for i, j in pairs])


def exchange(x, axis, bits):
    size = lax.axis_size(axis)
    return lax.ppermute(x, axis, [(i, i ^ bits) for i in range(size)])


def slots_kernel(
    side_ref,
    offsets_ref,
    count_ref,
    own_ref,
    row_a_ref,
    row_b_ref,
    col_a_ref,
    col_b_ref,
    corner_a_ref,
    corner_b_ref,
    probe_ref,
    patterns_ref,
    ahead_ref,
    back_ref,
    grad_ref,
    probe_grad_ref,
    padded,
    window,
    wave,
    half_ahead,
    far,
    weighted,
    half_back,
    chi,
    sems,
):
    tile = own_ref.shape[1]
    far_edge = tile + HALF
    row_odd = side_ref[0]
    col_odd = side_ref[1]
    row_a = pl.multiple_of((1 - row_odd) * far_edge, LANES)
    row_b = pl.multiple_of(row_odd * far_edge, LANES)
    col_a = pl.multiple_of((1 - col_odd) * far_edge, LANES)
    col_b = pl.multiple_of(col_odd * far_edge, LANES)
    middle = pl.ds(HALF, tile)
    moves = [
        (own_ref, middle, middle),
        (row_a_ref, pl.ds(row_a, HALF), middle),
        (row_b_ref, pl.ds(row_b, HALF), middle),
        (col_a_ref, middle, pl.ds(col_a, HALF)),
        (col_b_ref, middle, pl.ds(col_b, HALF)),
        (corner_a_ref.at[0], pl.ds(row_a, HALF), pl.ds(col_a, HALF)),
        (corner_a_ref.at[1], pl.ds(row_b, HALF), pl.ds(col_a, HALF)),
        (corner_b_ref.at[0], pl.ds(row_a, HALF), pl.ds(col_b, HALF)),
        (corner_b_ref.at[1], pl.ds(row_b, HALF), pl.ds(col_b, HALF)),
    ]
    copies = [
        pltpu.make_async_copy(source, padded.at[:, rows, columns], sems.at[index])
        for index, (source, rows, columns) in enumerate(moves)
    ]
    for copy in copies:
        copy.start()
    grad_ref[...] = jnp.zeros_like(grad_ref)
    probe_grad_ref[...] = jnp.zeros_like(probe_grad_ref)
    for copy in copies:
        copy.wait()
    lane = lax.broadcasted_iota(jnp.int32, (8, LANES), 1)
    sub = lax.broadcasted_iota(jnp.int32, (8, LANES), 0)
    zero = jnp.zeros((8, LANES), jnp.float32)
    step = 32

    def slot(k, carry):
        row = offsets_ref[0, k]
        column = offsets_ref[1, k]
        row_base = pl.multiple_of(row // 8 * 8, 8)
        row_shift = row - row_base
        col_base = pl.multiple_of(column // LANES * LANES, LANES)
        col_shift = column - col_base

        in_lane = lane < LANES - col_shift
        in_sub = sub < 8 - row_shift
        lane_turn = lax.rem(LANES - col_shift, LANES)
        sub_turn = lax.rem(8 - row_shift, 8)

        def lanes_of(plane, group):
            parts = [
                pltpu.roll(
                    padded[
                        plane, pl.ds(row_base + 8 * group, 8), pl.ds(col_base + LANES * j, LANES)
                    ],
                    lane_turn,
                    1,
                )
                for j in range(3)
            ]
            return [
                pltpu.roll(jnp.where(in_lane, parts[j], parts[j + 1]), sub_turn, 0)
                for j in range(2)
            ]

        for plane in range(2):
            before = lanes_of(plane, 0)
            for group in range(W // 8):
                after = lanes_of(plane, group + 1)
                for j in range(2):
                    window[plane, 8 * group : 8 * group + 8, LANES * j : LANES * j + LANES] = (
                        jnp.where(in_sub, before[j], after[j])
                    )
                before = after

        for mode in range(MODES):
            for start in range(0, W, step):
                rows = slice(start, start + step)
                object_real, object_imag = window[0, rows, :], window[1, rows, :]
                probe_real, probe_imag = probe_ref[0, mode, rows, :], probe_ref[1, mode, rows, :]
                into = slice(mode * W + start, mode * W + start + step)
                wave[into, :W] = (probe_real * object_real - probe_imag * object_imag).astype(
                    jnp.bfloat16
                )
                wave[into, W:] = (probe_real * object_imag + probe_imag * object_real).astype(
                    jnp.bfloat16
                )
        halfway = jnp.dot(
            wave[...], ahead_ref[...], preferred_element_type=jnp.float32
        ).astype(jnp.bfloat16)
        for mode in range(MODES):
            rows = slice(mode * W, mode * W + W)
            half_ahead[:W, rows] = halfway[rows, :W]
            half_ahead[W:, rows] = halfway[rows, W:]
        far[...] = jnp.dot(back_ref[...], half_ahead[...], preferred_element_type=jnp.float32)
        for start in range(0, W, step):
            rows = slice(start, start + step)
            imag_rows = slice(W + start, W + start + step)
            reals = [far[rows, m * W : m * W + W] for m in range(MODES)]
            imags = [far[imag_rows, m * W : m * W + W] for m in range(MODES)]
            intensity = sum(r * r + i * i for r, i in zip(reals, imags))
            residual = intensity - patterns_ref[k, rows, :].astype(jnp.float32)
            for m in range(MODES):
                into = slice(m * W + start, m * W + start + step)
                weighted[into, :W] = (residual * reals[m]).astype(jnp.bfloat16)
                weighted[into, W:] = (residual * imags[m]).astype(jnp.bfloat16)
        back_half = jnp.dot(
            weighted[...], back_ref[...], preferred_element_type=jnp.float32
        ).astype(jnp.bfloat16)
        for mode in range(MODES):
            rows = slice(mode * W, mode * W + W)
            half_back[:W, rows] = back_half[rows, :W]
            half_back[W:, rows] = back_half[rows, W:]
        chi[...] = jnp.dot(ahead_ref[...], half_back[...], preferred_element_type=jnp.float32)

        from_lane = lane >= col_shift
        from_sub = sub >= row_shift

        def terms(start, low):
            rows = slice(start, start + 8)
            imag_rows = slice(W + start, W + start + 8)
            columns = slice(low, low + LANES)
            object_real, object_imag = window[0, rows, columns], window[1, rows, columns]
            real, imag = zero, zero
            for m in range(MODES):
                at = slice(m * W + low, m * W + low + LANES)
                chi_real, chi_imag = chi[rows, at], chi[imag_rows, at]
                probe_real = probe_ref[0, m, rows, columns]
                probe_imag = probe_ref[1, m, rows, columns]
                probe_grad_ref[0, m, rows, columns] += (
                    object_real * chi_real + object_imag * chi_imag
                )
                probe_grad_ref[1, m, rows, columns] += (
                    object_real * chi_imag - object_imag * chi_real
                )
                real += probe_real * chi_real + probe_imag * chi_imag
                imag += probe_real * chi_imag - probe_imag * chi_real
            return [
                pltpu.roll(pltpu.roll(value, col_shift, 1), row_shift, 0) for value in (real, imag)
            ]

        before = [[zero, zero], [zero, zero]]
        for group in range(W // 8 + 1):
            if group < W // 8:
                after = [terms(8 * group, 0), terms(8 * group, LANES)]
            else:
                after = [[zero, zero], [zero, zero]]
            rows = pl.ds(row_base + 8 * group, 8)
            for plane in range(2):
                left = jnp.where(from_sub, after[0][plane], before[0][plane])
                right = jnp.where(from_sub, after[1][plane], before[1][plane])
                grad_ref[plane, rows, pl.ds(col_base, LANES)] += jnp.where(from_lane, left, 0.0)
                grad_ref[plane, rows, pl.ds(col_base + LANES, LANES)] += jnp.where(
                    from_lane, right, left
                )
                grad_ref[plane, rows, pl.ds(col_base + 2 * LANES, LANES)] += jnp.where(
                    from_lane, 0.0, right
                )
            before = after
        return carry

    lax.fori_loop(0, count_ref[0], slot, 0)


def slots(sides, offsets, count, own, halos, probe, patterns):
    tile = own.shape[1]
    rows = tile + 2 * HALF + 8
    columns = tile + 2 * HALF + LANES
    smem = pl.BlockSpec(memory_space=pltpu.SMEM)
    vmem = pl.BlockSpec(memory_space=pltpu.VMEM)
    anywhere = pl.BlockSpec(memory_space=pl.ANY)
    ahead, back = tables()
    square = (2 * W, 2 * W)
    return pl.pallas_call(
        slots_kernel,
        out_shape=(
            jax.ShapeDtypeStruct((2, rows, columns), jnp.float32),
            jax.ShapeDtypeStruct((2, MODES, W, W), jnp.float32),
        ),
        in_specs=[smem] * 3 + [anywhere] * 7 + [vmem] * 4,
        out_specs=(vmem, vmem),
        scratch_shapes=[
            pltpu.VMEM((2, rows, columns), jnp.float32),
            pltpu.VMEM((2, W, W), jnp.float32),
            pltpu.VMEM(square, jnp.bfloat16),
            pltpu.VMEM(square, jnp.bfloat16),
            pltpu.VMEM(square, jnp.float32),
            pltpu.VMEM(square, jnp.bfloat16),
            pltpu.VMEM(square, jnp.bfloat16),
            pltpu.VMEM(square, jnp.float32),
            pltpu.SemaphoreType.DMA((9,)),
        ],
        compiler_params=pltpu.CompilerParams(vmem_limit_bytes=50 * 1024 * 1024),
    )(sides, offsets, count, own, *halos, probe, patterns, jnp.asarray(ahead), jnp.asarray(back))


def cut(x, start, size, dim):
    return lax.dynamic_slice_in_dim(x, start, size, axis=dim)


def fold(total, axis):
    size = lax.axis_size(axis)
    me = lax.axis_index(axis)
    bits = 1
    while bits < size:
        mine = (me // bits) % 2
        half = total.shape[0] // 2
        keep = cut(total, mine * half, half, 0)
        away = cut(total, (1 - mine) * half, half, 0)
        total = keep + exchange(away, axis, bits)
        bits *= 2
    return total


def unfold(part, axis):
    size = lax.axis_size(axis)
    me = lax.axis_index(axis)
    bits = size // 2
    while bits:
        mine = (me // bits) % 2
        other = exchange(part, axis, bits)
        part = jnp.where(
            mine == 0, jnp.concatenate([part, other]), jnp.concatenate([other, part])
        )
        bits //= 2
    return part


def summed(value, axes):
    for axis in axes:
        bits = 1
        while bits < lax.axis_size(axis):
            value = value + exchange(value, axis, bits)
            bits *= 2
    return value


def local(object_field, probe, positions, counts, patterns):
    tile = object_field.shape[1]
    edge = tile - HALF
    row_odd = lax.axis_index("row") % 2
    col_odd = lax.axis_index("col") % 2
    live = counts[0, 0]

    row_a = swap(cut(object_field, (1 - row_odd) * edge, HALF, 1), "row", 0)
    row_b = swap(cut(object_field, row_odd * edge, HALF, 1), "row", 1)
    col_a = swap(cut(object_field, (1 - col_odd) * edge, HALF, 2), "col", 0)
    col_b = swap(cut(object_field, col_odd * edge, HALF, 2), "col", 1)
    both = jnp.stack([row_a, row_b])
    corner_a = swap(cut(both, (1 - col_odd) * edge, HALF, 3), "col", 0)
    corner_b = swap(cut(both, col_odd * edge, HALF, 3), "col", 1)
    count = jnp.full((8, LANES), live.astype(jnp.float32))
    total_count = summed(count, ("col", "row"))[0, 0]

    sides = jnp.stack([row_odd, col_odd]).astype(jnp.int32)
    grad, probe_part = slots(
        sides,
        positions[0, 0],
        live[None],
        object_field,
        (row_a, row_b, col_a, col_b, corner_a, corner_b),
        probe,
        patterns[0, 0],
    )

    far_edge = tile + HALF
    top, bottom = grad[:, :HALF], grad[:, far_edge : far_edge + HALF]
    outer = jnp.stack([top, bottom])
    inner = grad[:, HALF:far_edge]
    corner_a = swap(cut(outer, (1 - col_odd) * far_edge, HALF, 3), "col", 0)
    corner_b = swap(cut(outer, col_odd * far_edge, HALF, 3), "col", 1)
    col_a = swap(cut(inner, (1 - col_odd) * far_edge, HALF, 2), "col", 0)
    col_b = swap(cut(inner, col_odd * far_edge, HALF, 2), "col", 1)
    left = jnp.where(col_odd == 1, corner_a, corner_b)
    right = jnp.where(col_odd == 1, corner_b, corner_a)
    outer = outer[..., HALF:far_edge]
    outer = outer.at[..., :HALF].add(left).at[..., edge:].add(right)
    row_a = swap(jnp.where(row_odd == 1, outer[0], outer[1]), "row", 0)
    row_b = swap(jnp.where(row_odd == 1, outer[1], outer[0]), "row", 1)
    result = inner[:, :, HALF:far_edge]
    left = jnp.where(col_odd == 1, col_a, col_b)
    right = jnp.where(col_odd == 1, col_b, col_a)
    result = result.at[:, :, :HALF].add(left).at[:, :, edge:].add(right)
    above = jnp.where(row_odd == 1, row_a, row_b)
    below = jnp.where(row_odd == 1, row_b, row_a)
    result = result.at[:, :HALF].add(above).at[:, edge:].add(below)

    flat = probe_part.reshape(-1, W)
    part = fold(fold(flat, "col"), "row")
    whole = unfold(unfold(part, "row"), "col")
    return result, whole.reshape(probe.shape) / total_count


def solution(mesh):
    placed = (
        P(None, ("groups", "row"), "col"),
        P(None, "groups", None, None),
        P(("groups", "row"), "col", None, None),
        P(("groups", "row"), "col"),
        P(("groups", "row"), "col", None, None, None),
    )
    return jax.shard_map(
        local,
        mesh=mesh,
        in_specs=placed,
        out_specs=(P(None, ("groups", "row"), "col"), P(None, "groups", None, None)),
        check_vma=False,
    )
```

time: 387 us -> 116 us (0.30); the launches traced: 381 us -> 116 us
  local copies, waits for them, and re-layouts: 91.9 us -> 7.77 us
  other arithmetic: 82.2 us -> 3.62 us
  blocking collectives: 42.6 us -> 0 us
  starting transfers between devices: 20.4 us -> 57.8 us
  matrix products: 32 us -> 0 us
  loops' own time: 30.3 us -> 0 us
  waiting for transfers between devices: 66.9 us -> 37 us
  between operations: 14.9 us -> 1.71 us
  Pallas kernels: 0 us -> 7.81 us
    dynamic_update_slice x8 -> x0, local copies, waits for them, and re-layouts: 51.9 us -> none  [one_block(): lax.dynamic_update_slice(gradient, current + object_terms[slot_index], co...]
    psum x1 -> x0, waiting for transfers between devices: 43.9 us -> none  [local(): lax.psum((probe_total, count_here), ('col', 'row'))]
    psum x1 -> x0, blocking collectives: 42.6 us -> none  [local(): lax.psum((probe_total, count_here), ('col', 'row'))]
    ppermute x8 -> x24, starting transfers between devices: 20.3 us -> 57.8 us  [the longest x12 30.9 us: swap(): return lax.ppermute(x, axis, pairs + [(j, i) for i, j in pairs])]
    dot_general x24 -> x0, matrix products: 32 us -> none  [the longest x8 11.2 us: transform(): jnp.einsum('jk,bkx->bjx', sine_table, halfway, preferred_element_type=jnp...]
    another operation x1 -> x0, loops' own time: 30.3 us -> none  [local(): gradient, probe_total = lax.fori_loop(0, block_count, one_block, start)]
    add x16 -> x8, other arithmetic: 26.3 us -> 0.15 us  [the longest x4 0.14 us: fold(): total = keep + exchange(away, axis, bits)]
    reduce_sum x8 -> x0, other arithmetic: 14.8 us -> none  [the longest x4 13.5 us: one_block(): jnp.sum(object_real * back_real + object_imag * back_imag, axis=0)]
  transfers between devices with their start and end apart: 9 -> 24, of which waited for: 7 -> 11; matrix products, arithmetic and copies ran while one was open for 3% -> 6% of each run, Pallas kernels for 0% -> 7%
where the time goes in v1:
time: 116 us
  starting transfers between devices  57.8 us (50%)
  waiting for transfers between devices  37 us (32%)
  Pallas kernels  7.81 us (7%)
  local copies, waits for them, and re-layouts  7.77 us (7%)
  other arithmetic  3.62 us (3%)
  between operations  1.71 us (1%)
    ppermute x12, starting transfers between devices, swap(): return lax.ppermute(x, axis, pairs + [(j, i) for i, j in pairs])  30.9 us
    ppermute x12, waiting for transfers between devices, exchange(): return lax.ppermute(x, axis, [(i, i ^ bits) for i in range(size)])  29.9 us
    ppermute x12, starting transfers between devices, exchange(): return lax.ppermute(x, axis, [(i, i ^ bits) for i in range(size)])  26.9 us
    pallas_call x1, Pallas kernels, slots(): pl.pallas_call(slots_kernel, out_shape=(jax.ShapeDtypeStruct((2, rows, co...  7.81 us
    ppermute x12, waiting for transfers between devices, swap(): return lax.ppermute(x, axis, pairs + [(j, i) for i, j in pairs])  7.08 us
    dynamic_slice x7, local copies, waits for them, and re-layouts, cut(): return lax.dynamic_slice_in_dim(x, start, size, axis=dim)  4.17 us
  transfers between devices with their start and end apart: 24, of which 11 were waited for; matrix products, arithmetic and copies ran while one was open for 6% of the time, Pallas kernels for 7%

profile of v1, /device:TPU:5, one launch (start us, length us, event | category | flops | bytes accessed | tf_op | source)
XLA Modules:
  0.0 115.7 jit_solution(313753754775087015)
XLA Ops:
  0.7 2.0 %constant_dynamic-slice_fusion.8 = (f32[2,128,384]{2,1,0:T(8,128)S(1)}, f32[2,128,384]{2,1,0:T(8,128)}) fusion(f32[2,384,384]{2,1,0:T(8,128)} %own_ref.1, s32[]{:T(128)S(6)} %select_n.179, s32[]{:T(128)S(6)} %select_n.178), kind=kLoop, calls=%fused_computation.50 | loop fusion | bytes 1572872 | tf_op jit(solution)/shard_map/dynamic_slice | solution.py:265
  2.7 1.3 %collective-permute-start = (f32[2,128,384]{2,1,0:T(8,128)}, f32[2,128,384]{2,1,0:T(8,128)S(1)}, u32[]{:S(2)}, u32[]{:S(2)}) collective-permute-start(f32[2,128,384]{2,1,0:T(8,128)} %get-tuple-element.87), channel_id=1, source_target_pairs={{0,1},{2,3},{1,0},{3,2},{4,5},{6,7},{5,4},{7,6},{8,9},{10,11},{9,8... | collective-permute-start | bytes 1179656 | tf_op jit(solution)/shard_map/ppermute | solution.py:34
  4.0 0.7 collective-permute-start.1
  4.7 1.0 constant_dynamic-slice_fusion.6
  5.7 1.0 collective-permute-start.2
  6.6 3.0 %collective-permute-start.3 = (f32[2,384,128]{2,1,0:T(8,128)}, f32[2,384,128]{2,1,0:T(8,128)S(1)}, u32[]{:S(2)}, u32[]{:S(2)}) collective-permute-start(f32[2,384,128]{2,1,0:T(8,128)} %get-tuple-element.84), channel_id=1, source_target_pairs={{4,8},{8,4},{5,9},{9,5},{6,10},{10,6},{7,11},{11,7},{20,24},{24,20... | collective-permute-start | bytes 1179656 | tf_op jit(solution)/shard_map/ppermute | solution.py:34
  10.3 0.1 collective-permute-start.20
  10.4 2.5 %collective-permute-done.row_a_ref = f32[2,128,384]{2,1,0:T(8,128)S(1)} collective-permute-done((f32[2,128,384]{2,1,0:T(8,128)}, f32[2,128,384]{2,1,0:T(8,128)S(1)}, u32[]{:S(2)}, u32[]{:S(2)}) %collective-permute-start) | collective-permute-done | bytes 393248 | tf_op jit(solution)/shard_map/ppermute | solution.py:34
  12.9 0.7 fusion.5
  13.6 1.5 %collective-permute-start.4 = (f32[2,2,128,128]{3,2,1,0:T(8,128)}, f32[2,2,128,128]{3,2,1,0:T(8,128)S(1)}, u32[]{:S(2)}, u32[]{:S(2)}) collective-permute-start(f32[2,2,128,128]{3,2,1,0:T(8,128)} %get-tuple-element.91), channel_id=1, source_target_pairs={{0,4},{8,12},{4,0},{12,8},{1,5},{9,13},{5,1},{13,9},{2,6},{10,14},... | collective-permute-start | bytes 786440 | tf_op jit(solution)/shard_map/ppermute | solution.py:34
  15.2 3.0 %collective-permute-start.5 = (f32[2,2,128,128]{3,2,1,0:T(8,128)S(1)}, f32[2,2,128,128]{3,2,1,0:T(8,128)S(1)}, u32[]{:S(2)}, u32[]{:S(2)}) collective-permute-start(f32[2,2,128,128]{3,2,1,0:T(8,128)S(1)} %get-tuple-element.90), channel_id=1, source_target_pairs={{4,8},{8,4},{5,9},{9,5},{6,10},{10,6},{7,11},{11,7},{20,24},{24,20... | collective-permute-start | bytes 786440 | tf_op jit(solution)/shard_map/ppermute | solution.py:34
  18.2 0.1 pad_add_fusion.side_ref
  18.3 4.6 %collective-permute-done.5.corner_b_ref = f32[2,2,128,128]{3,2,1,0:T(8,128)S(1)} collective-permute-done((f32[2,2,128,128]{3,2,1,0:T(8,128)S(1)}, f32[2,2,128,128]{3,2,1,0:T(8,128)S(1)}, u32[]{:S(2)}, u32[]{:S(2)}) %collective-permute-start.5) | collective-permute-done | bytes 262176 | tf_op jit(solution)/shard_map/ppermute | solution.py:34
  22.9 7.8 %shard_map.86 = (f32[2,648,768]{2,1,0:T(8,128)}, f32[2,2,256,256]{3,2,1,0:T(8,128)}) custom-call(s32[2]{0:T(128)S(1)} %pad_add_fusion.side_ref, s32[2,8]{1,0:T(2,128)S(1)} %bitcast.22, s32[1]{0:T(128)} %bitcast.19.count_ref, f32[2,384,384]{2,1,0:T(8,128)} %own_ref.1, f32[2,128,384]{2,1,0:T(8,128)S(1)} %collective-permute-done.row_a_ref, ...), custom_call_target="tpu_custom_call" | custom-call | tf_op jit(solution)/shard_map/pallas_call | solution.py:241
  30.7 1.1 constant_dynamic-slice_fusion.3
  31.9 12.0 %collective-permute-start.22 = (f32[8,128]{1,0:T(8,128)S(1)}, f32[8,128]{1,0:T(8,128)S(1)}, u32[]{:S(2)}, u32[]{:S(2)}) collective-permute-start(f32[8,128]{1,0:T(8,128)S(1)} %fusion.13), channel_id=1, source_target_pairs={{0,1},{1,0},{2,3},{3,2},{4,5},{5,4},{6,7},{7,6},{8,9},{9,8},{10,11... | collective-permute-start | bytes 12296 | tf_op jit(solution)/shard_map/ppermute | solution.py:39
  43.9 1.0 collective-permute-done.22
  44.9 3.3 %collective-permute-done.23 = f32[8,128]{1,0:T(8,128)S(1)} collective-permute-done((f32[8,128]{1,0:T(8,128)S(1)}, f32[8,128]{1,0:T(8,128)S(1)}, u32[]{:S(2)}, u32[]{:S(2)}) %collective-permute-start.23) | collective-permute-done | bytes 4128 | tf_op jit(solution)/shard_map/ppermute | solution.py:39
  48.2 0.5 slice.196
  48.7 2.0 %slice.185 = f32[2,384,768]{2,1,0:T(8,128)S(1)} slice(f32[2,648,768]{2,1,0:T(8,128)} %get-tuple-element.76), slice={[0:2], [128:512], [0:768]} | slice | bytes 4718592 | tf_op jit(solution)/shard_map/slice | solution.py:336
  50.7 0.9 copy-done.3
  51.6 0.1 slice.183
  51.7 0.1 slice_bitcast_fusion
  51.9 2.5 %collective-permute-start.8 = (f32[2,2,128,128]{3,2,1,0:T(8,128)S(1)}, f32[2,2,128,128]{3,2,1,0:T(8,128)S(1)}, u32[]{:S(2)}, u32[]{:S(2)}) collective-permute-start(f32[2,2,128,128]{3,2,1,0:T(8,128)S(1)} %get-tuple-element.83), channel_id=1, source_target_pairs={{0,4},{8,12},{4,0},{12,8},{1,5},{9,13},{5,1},{13,9},{2,6},{10,14},... | collective-permute-start | bytes 786440 | tf_op jit(solution)/shard_map/ppermute | solution.py:34
  54.4 13.4 %collective-permute-start.9 = (f32[2,2,128,128]{3,2,1,0:T(8,128)S(1)}, f32[2,2,128,128]{3,2,1,0:T(8,128)S(1)}, u32[]{:S(2)}, u32[]{:S(2)}) collective-permute-start(f32[2,2,128,128]{3,2,1,0:T(8,128)S(1)} %get-tuple-element.82), channel_id=1, source_target_pairs={{4,8},{8,4},{5,9},{9,5},{6,10},{10,6},{7,11},{11,7},{20,24},{24,20... | collective-permute-start | bytes 786440 | tf_op jit(solution)/shard_map/ppermute | solution.py:34
  67.8 0.1 dynamic-slice_add_fusion
  68.0 0.4 collective-permute-start.6
  68.5 3.4 %collective-permute-start.7 = (f32[2,384,128]{2,1,0:T(8,128)S(1)}, f32[2,384,128]{2,1,0:T(8,128)S(1)}, u32[]{:S(2)}, u32[]{:S(2)}) collective-permute-start(f32[2,384,128]{2,1,0:T(8,128)S(1)} %get-tuple-element.80), channel_id=1, source_target_pairs={{4,8},{8,4},{5,9},{9,5},{6,10},{10,6},{7,11},{11,7},{20,24},{24,20... | collective-permute-start | bytes 1179656 | tf_op jit(solution)/shard_map/ppermute | solution.py:34
  71.9 4.8 %collective-permute-done.13 = f32[256,256]{1,0:T(8,128)S(1)} collective-permute-done((f32[256,256]{1,0:T(8,128)S(1)}, f32[256,256]{1,0:T(8,128)S(1)}, u32[]{:S(2)}, u32[]{:S(2)}) %collective-permute-start.13) | collective-permute-done | bytes 262176 | tf_op jit(solution)/shard_map/ppermute | solution.py:39
  76.7 0.1 collective-permute-start.14
  76.9 3.7 %collective-permute-done.14 = f32[128,256]{1,0:T(8,128)S(1)} collective-permute-done((f32[128,256]{1,0:T(8,128)S(1)}, f32[128,256]{1,0:T(8,128)S(1)}, u32[]{:S(2)}, u32[]{:S(2)}) %collective-permute-start.14) | collective-permute-done | bytes 131104 | tf_op jit(solution)/shard_map/ppermute | solution.py:39
  80.6 2.7 %collective-permute-start.15 = (f32[64,256]{1,0:T(8,128)S(1)}, f32[64,256]{1,0:T(8,128)S(1)}, u32[]{:S(2)}, u32[]{:S(2)}) collective-permute-start(f32[64,256]{1,0:T(8,128)S(1)} %constant_dynamic-slice_fusion), channel_id=1, source_target_pairs={{0,2},{1,3},{2,0},{3,1},{4,6},{5,7},{6,4},{7,5},{8,10},{9,11},{10,... | collective-permute-start | bytes 196616 | tf_op jit(solution)/shard_map/ppermute | solution.py:39
  83.3 0.1 fusion.12
  83.5 2.1 %collective-permute-done.15 = f32[64,256]{1,0:T(8,128)S(1)} collective-permute-done((f32[64,256]{1,0:T(8,128)S(1)}, f32[64,256]{1,0:T(8,128)S(1)}, u32[]{:S(2)}, u32[]{:S(2)}) %collective-permute-start.15) | collective-permute-done | bytes 65568 | tf_op jit(solution)/shard_map/ppermute | solution.py:39
  85.6 1.9 %collective-permute-start.16 = (f32[64,256]{1,0:T(8,128)S(1)}, f32[64,256]{1,0:T(8,128)S(1)}, u32[]{:S(2)}, u32[]{:S(2)}) collective-permute-start(f32[64,256]{1,0:T(8,128)S(1)} %dynamic-slice_add_fusion.3), channel_id=1, source_target_pairs={{0,2},{1,3},{2,0},{3,1},{4,6},{5,7},{6,4},{7,5},{8,10},{9,11},{10,... | collective-permute-start | bytes 196616 | tf_op jit(solution)/shard_map/ppermute | solution.py:39
  87.6 0.7 collective-permute-start.11
  88.3 1.9 %collective-permute-done.16 = f32[64,256]{1,0:T(8,128)S(1)} collective-permute-done((f32[64,256]{1,0:T(8,128)S(1)}, f32[64,256]{1,0:T(8,128)S(1)}, u32[]{:S(2)}, u32[]{:S(2)}) %collective-permute-start.16) | collective-permute-done | bytes 65568 | tf_op jit(solution)/shard_map/ppermute | solution.py:39
  90.2 0.9 collective-permute-start.17
  91.1 0.1 add_dynamic-update-slice_fusion
  91.1 6.4 %collective-permute-done.17 = f32[128,256]{1,0:T(8,128)S(1)} collective-permute-done((f32[128,256]{1,0:T(8,128)S(1)}, f32[128,256]{1,0:T(8,128)S(1)}, u32[]{:S(2)}, u32[]{:S(2)}) %collective-permute-start.17) | collective-permute-done | bytes 131104 | tf_op jit(solution)/shard_map/ppermute | solution.py:39
  97.6 7.5 %collective-permute-start.18 = (f32[256,256]{1,0:T(8,128)S(1)}, f32[256,256]{1,0:T(8,128)S(1)}, u32[]{:S(2)}, u32[]{:S(2)}) collective-permute-start(f32[256,256]{1,0:T(8,128)S(1)} %maximum_select_fusion.2), channel_id=1, source_target_pairs={{0,8},{4,12},{8,0},{12,4},{1,9},{5,13},{9,1},{13,5},{2,10},{6,14},... | collective-permute-start | bytes 786440 | tf_op jit(solution)/shard_map/ppermute | solution.py:39
  105.1 0.1 fusion.4
  105.2 5.5 %collective-permute-done.18 = f32[256,256]{1,0:T(8,128)S(1)} collective-permute-done((f32[256,256]{1,0:T(8,128)S(1)}, f32[256,256]{1,0:T(8,128)S(1)}, u32[]{:S(2)}, u32[]{:S(2)}) %collective-permute-start.18) | collective-permute-done | bytes 262176 | tf_op jit(solution)/shard_map/ppermute | solution.py:39
  110.7 1.7 %collective-permute-start.19 = (f32[512,256]{1,0:T(8,128)S(1)}, f32[512,256]{1,0:T(8,128)S(1)}, u32[]{:S(2)}, u32[]{:S(2)}) collective-permute-start(f32[512,256]{1,0:T(8,128)S(1)} %maximum_select_fusion.1), channel_id=1, source_target_pairs={{0,4},{4,0},{8,12},{12,8},{1,5},{5,1},{9,13},{13,9},{2,6},{6,2},{1... | collective-permute-start | bytes 1572872 | tf_op jit(solution)/shard_map/ppermute | solution.py:39
  112.5 0.1 fusion.3
  112.6 0.1 fusion.2
  112.8 1.2 %collective-permute-done.19 = f32[512,256]{1,0:T(8,128)S(1)} collective-permute-done((f32[512,256]{1,0:T(8,128)S(1)}, f32[512,256]{1,0:T(8,128)S(1)}, u32[]{:S(2)}, u32[]{:S(2)}) %collective-permute-start.19) | collective-permute-done | bytes 524320 | tf_op jit(solution)/shard_map/ppermute | solution.py:39
  114.0 1.7 %fusion = f32[1024,256]{1,0:T(8,128)} fusion(f32[512,256]{1,0:T(8,128)S(1)} %collective-permute-done.19, f32[512,256]{1,0:T(8,128)S(1)} %maximum_select_fusion.1, f32[]{:T(128)} %bitcast.13, pred[]{:T(512)S(6)} %eq.37), kind=kLoop, calls=%fused_computation.9 | loop fusion | flops 1048576 | bytes 2097157 | tf_op jit(solution)/shard_map/div | solution.py:358
  (50 shorter events, 0.8 us)
Async XLA Ops:
  0.6 4.1 %copy-start.4 = (f32[2,384,384]{2,1,0:T(8,128)S(1)}, f32[2,384,384]{2,1,0:T(8,128)}, u32[]{:S(2)}) copy-start(f32[2,384,384]{2,1,0:T(8,128)} %own_ref.1) | copy-start | bytes 3538948
  2.7 10.2 %collective-permute-start = (f32[2,128,384]{2,1,0:T(8,128)}, f32[2,128,384]{2,1,0:T(8,128)S(1)}, u32[]{:S(2)}, u32[]{:S(2)}) collective-permute-start(f32[2,128,384]{2,1,0:T(8,128)} %get-tuple-element.87), channel_id=1, source_target_pairs={{0,1},{2,3},{1,0},{3,2},{4,5},{6,7},{5,4},{7,6},{8,9},{10,11},{9,8... | collective-permute-start | bytes 1179656 | tf_op jit(solution)/shard_map/ppermute | solution.py:34
  4.0 8.9 %collective-permute-start.1 = (f32[2,128,384]{2,1,0:T(8,128)S(1)}, f32[2,128,384]{2,1,0:T(8,128)S(1)}, u32[]{:S(2)}, u32[]{:S(2)}) collective-permute-start(f32[2,128,384]{2,1,0:T(8,128)S(1)} %get-tuple-element.86), channel_id=1, source_target_pairs={{1,2},{2,1},{5,6},{6,5},{9,10},{10,9},{13,14},{14,13},{17,18},{18,... | collective-permute-start | bytes 1179656 | tf_op jit(solution)/shard_map/ppermute | solution.py:34
  4.7 18.2 %copy-start = (bf16[512,512]{1,0:T(8,128)(2,1)S(1)}, bf16[512,512]{1,0:T(8,128)(2,1)}, u32[]{:S(2)}) copy-start(bf16[512,512]{1,0:T(8,128)(2,1)} %constant.264.clone.ahead_ref) | copy-start | bytes 1572868
  4.7 18.2 %copy-start.1 = (bf16[512,512]{1,0:T(8,128)(2,1)S(1)}, bf16[512,512]{1,0:T(8,128)(2,1)}, u32[]{:S(2)}) copy-start(bf16[512,512]{1,0:T(8,128)(2,1)} %constant.265.clone.back_ref) | copy-start | bytes 1572868
  4.7 18.2 %copy-start.2 = (s32[1,1,2,8]{3,2,1,0:T(2,128)S(1)}, s32[1,1,2,8]{3,2,1,0:T(2,128)}, u32[]{:S(2)}) copy-start(s32[1,1,2,8]{3,2,1,0:T(2,128)} %param.21) | copy-start | bytes 196
  5.7 12.6 %collective-permute-start.2 = (f32[2,384,128]{2,1,0:T(8,128)}, f32[2,384,128]{2,1,0:T(8,128)S(1)}, u32[]{:S(2)}, u32[]{:S(2)}) collective-permute-start(f32[2,384,128]{2,1,0:T(8,128)} %get-tuple-element.85), channel_id=1, source_target_pairs={{0,4},{8,12},{4,0},{12,8},{1,5},{9,13},{5,1},{13,9},{2,6},{10,14},... | collective-permute-start | bytes 1179656 | tf_op jit(solution)/shard_map/ppermute | solution.py:34
  6.6 11.7 %collective-permute-start.3 = (f32[2,384,128]{2,1,0:T(8,128)}, f32[2,384,128]{2,1,0:T(8,128)S(1)}, u32[]{:S(2)}, u32[]{:S(2)}) collective-permute-start(f32[2,384,128]{2,1,0:T(8,128)} %get-tuple-element.84), channel_id=1, source_target_pairs={{4,8},{8,4},{5,9},{9,5},{6,10},{10,6},{7,11},{11,7},{20,24},{24,20... | collective-permute-start | bytes 1179656 | tf_op jit(solution)/shard_map/ppermute | solution.py:34
  10.3 7.9 %collective-permute-start.20 = (f32[8,128]{1,0:T(8,128)S(1)}, f32[8,128]{1,0:T(8,128)S(1)}, u32[]{:S(2)}, u32[]{:S(2)}) collective-permute-start(f32[8,128]{1,0:T(8,128)S(1)} %broadcast_in_dim.3), channel_id=1, source_target_pairs={{0,4},{4,0},{8,12},{12,8},{1,5},{5,1},{9,13},{13,9},{2,6},{6,2},{1... | collective-permute-start | bytes 12296 | tf_op jit(solution)/shard_map/ppermute | solution.py:39
  13.6 4.7 %collective-permute-start.4 = (f32[2,2,128,128]{3,2,1,0:T(8,128)}, f32[2,2,128,128]{3,2,1,0:T(8,128)S(1)}, u32[]{:S(2)}, u32[]{:S(2)}) collective-permute-start(f32[2,2,128,128]{3,2,1,0:T(8,128)} %get-tuple-element.91), channel_id=1, source_target_pairs={{0,4},{8,12},{4,0},{12,8},{1,5},{9,13},{5,1},{13,9},{2,6},{10,14},... | collective-permute-start | bytes 786440 | tf_op jit(solution)/shard_map/ppermute | solution.py:34
  15.2 7.7 %collective-permute-start.5 = (f32[2,2,128,128]{3,2,1,0:T(8,128)S(1)}, f32[2,2,128,128]{3,2,1,0:T(8,128)S(1)}, u32[]{:S(2)}, u32[]{:S(2)}) collective-permute-start(f32[2,2,128,128]{3,2,1,0:T(8,128)S(1)} %get-tuple-element.90), channel_id=1, source_target_pairs={{4,8},{8,4},{5,9},{9,5},{6,10},{10,6},{7,11},{11,7},{20,24},{24,20... | collective-permute-start | bytes 786440 | tf_op jit(solution)/shard_map/ppermute | solution.py:34
  18.2 13.6 %collective-permute-start.21 = (f32[8,128]{1,0:T(8,128)S(1)}, f32[8,128]{1,0:T(8,128)S(1)}, u32[]{:S(2)}, u32[]{:S(2)}) collective-permute-start(f32[8,128]{1,0:T(8,128)S(1)} %broadcast_add_fusion), channel_id=1, source_target_pairs={{0,8},{4,12},{8,0},{12,4},{1,9},{5,13},{9,1},{13,5},{2,10},{6,14},... | collective-permute-start | bytes 12296 | tf_op jit(solution)/shard_map/ppermute | solution.py:39
  31.8 35.9 %collective-permute-start.12 = (f32[512,256]{1,0:T(8,128)S(1)}, f32[512,256]{1,0:T(8,128)S(1)}, u32[]{:S(2)}, u32[]{:S(2)}) collective-permute-start(f32[512,256]{1,0:T(8,128)S(1)} %constant_dynamic-slice_fusion.3), channel_id=1, source_target_pairs={{0,4},{4,0},{8,12},{12,8},{1,5},{5,1},{9,13},{13,9},{2,6},{6,2},{1... | collective-permute-start | bytes 1572872 | tf_op jit(solution)/shard_map/ppermute | solution.py:39
  31.9 13.0 %collective-permute-start.22 = (f32[8,128]{1,0:T(8,128)S(1)}, f32[8,128]{1,0:T(8,128)S(1)}, u32[]{:S(2)}, u32[]{:S(2)}) collective-permute-start(f32[8,128]{1,0:T(8,128)S(1)} %fusion.13), channel_id=1, source_target_pairs={{0,1},{1,0},{2,3},{3,2},{4,5},{5,4},{6,7},{7,6},{8,9},{9,8},{10,11... | collective-permute-start | bytes 12296 | tf_op jit(solution)/shard_map/ppermute | solution.py:39
  44.9 3.4 %collective-permute-start.23 = (f32[8,128]{1,0:T(8,128)S(1)}, f32[8,128]{1,0:T(8,128)S(1)}, u32[]{:S(2)}, u32[]{:S(2)}) collective-permute-start(f32[8,128]{1,0:T(8,128)S(1)} %add.165), channel_id=1, source_target_pairs={{0,2},{1,3},{2,0},{3,1},{4,6},{5,7},{6,4},{7,5},{8,10},{9,11},{10,... | collective-permute-start | bytes 12296 | tf_op jit(solution)/shard_map/ppermute | solution.py:39
  48.7 2.8 %copy-start.3 = (f32[2,648,768]{2,1,0:T(8,128)S(1)}, f32[2,648,768]{2,1,0:T(8,128)}, u32[]{:S(2)}) copy-start(f32[2,648,768]{2,1,0:T(8,128)} %get-tuple-element.76) | copy-start | bytes 11943940
  51.8 16.0 %copy-start.6 = (f32[2,2,256,256]{3,2,1,0:T(8,128)S(1)}, f32[2,2,256,256]{3,2,1,0:T(8,128)}, u32[]{:S(2)}) copy-start(f32[2,2,256,256]{3,2,1,0:T(8,128)} %get-tuple-element.77) | copy-start | bytes 3145732
  51.9 24.9 %collective-permute-start.8 = (f32[2,2,128,128]{3,2,1,0:T(8,128)S(1)}, f32[2,2,128,128]{3,2,1,0:T(8,128)S(1)}, u32[]{:S(2)}, u32[]{:S(2)}) collective-permute-start(f32[2,2,128,128]{3,2,1,0:T(8,128)S(1)} %get-tuple-element.83), channel_id=1, source_target_pairs={{0,4},{8,12},{4,0},{12,8},{1,5},{9,13},{5,1},{13,9},{2,6},{10,14},... | collective-permute-start | bytes 786440 | tf_op jit(solution)/shard_map/ppermute | solution.py:34
  54.4 22.5 %collective-permute-start.9 = (f32[2,2,128,128]{3,2,1,0:T(8,128)S(1)}, f32[2,2,128,128]{3,2,1,0:T(8,128)S(1)}, u32[]{:S(2)}, u32[]{:S(2)}) collective-permute-start(f32[2,2,128,128]{3,2,1,0:T(8,128)S(1)} %get-tuple-element.82), channel_id=1, source_target_pairs={{4,8},{8,4},{5,9},{9,5},{6,10},{10,6},{7,11},{11,7},{20,24},{24,20... | collective-permute-start | bytes 786440 | tf_op jit(solution)/shard_map/ppermute | solution.py:34
  67.9 8.8 %collective-permute-start.13 = (f32[256,256]{1,0:T(8,128)S(1)}, f32[256,256]{1,0:T(8,128)S(1)}, u32[]{:S(2)}, u32[]{:S(2)}) collective-permute-start(f32[256,256]{1,0:T(8,128)S(1)} %constant_dynamic-slice_fusion.2), channel_id=1, source_target_pairs={{0,8},{4,12},{8,0},{12,4},{1,9},{5,13},{9,1},{13,5},{2,10},{6,14},... | collective-permute-start | bytes 786440 | tf_op jit(solution)/shard_map/ppermute | solution.py:39
  68.0 23.0 %collective-permute-start.6 = (f32[2,384,128]{2,1,0:T(8,128)S(1)}, f32[2,384,128]{2,1,0:T(8,128)S(1)}, u32[]{:S(2)}, u32[]{:S(2)}) collective-permute-start(f32[2,384,128]{2,1,0:T(8,128)S(1)} %get-tuple-element.81), channel_id=1, source_target_pairs={{0,4},{8,12},{4,0},{12,8},{1,5},{9,13},{5,1},{13,9},{2,6},{10,14},... | collective-permute-start | bytes 1179656 | tf_op jit(solution)/shard_map/ppermute | solution.py:34
  68.5 22.6 %collective-permute-start.7 = (f32[2,384,128]{2,1,0:T(8,128)S(1)}, f32[2,384,128]{2,1,0:T(8,128)S(1)}, u32[]{:S(2)}, u32[]{:S(2)}) collective-permute-start(f32[2,384,128]{2,1,0:T(8,128)S(1)} %get-tuple-element.80), channel_id=1, source_target_pairs={{4,8},{8,4},{5,9},{9,5},{6,10},{10,6},{7,11},{11,7},{20,24},{24,20... | collective-permute-start | bytes 1179656 | tf_op jit(solution)/shard_map/ppermute | solution.py:34
  76.7 3.9 %collective-permute-start.14 = (f32[128,256]{1,0:T(8,128)S(1)}, f32[128,256]{1,0:T(8,128)S(1)}, u32[]{:S(2)}, u32[]{:S(2)}) collective-permute-start(f32[128,256]{1,0:T(8,128)S(1)} %constant_dynamic-slice_fusion.1), channel_id=1, source_target_pairs={{0,1},{1,0},{2,3},{3,2},{4,5},{5,4},{6,7},{7,6},{8,9},{9,8},{10,11... | collective-permute-start | bytes 393224 | tf_op jit(solution)/shard_map/ppermute | solution.py:39
  80.6 4.9 %collective-permute-start.15 = (f32[64,256]{1,0:T(8,128)S(1)}, f32[64,256]{1,0:T(8,128)S(1)}, u32[]{:S(2)}, u32[]{:S(2)}) collective-permute-start(f32[64,256]{1,0:T(8,128)S(1)} %constant_dynamic-slice_fusion), channel_id=1, source_target_pairs={{0,2},{1,3},{2,0},{3,1},{4,6},{5,7},{6,4},{7,5},{8,10},{9,11},{10,... | collective-permute-start | bytes 196616 | tf_op jit(solution)/shard_map/ppermute | solution.py:39
  85.6 4.6 %collective-permute-start.16 = (f32[64,256]{1,0:T(8,128)S(1)}, f32[64,256]{1,0:T(8,128)S(1)}, u32[]{:S(2)}, u32[]{:S(2)}) collective-permute-start(f32[64,256]{1,0:T(8,128)S(1)} %dynamic-slice_add_fusion.3), channel_id=1, source_target_pairs={{0,2},{1,3},{2,0},{3,1},{4,6},{5,7},{6,4},{7,5},{8,10},{9,11},{10,... | collective-permute-start | bytes 196616 | tf_op jit(solution)/shard_map/ppermute | solution.py:39
  87.5 25.0 %collective-permute-start.10 = (f32[2,128,384]{2,1,0:T(8,128)S(1)}, f32[2,128,384]{2,1,0:T(8,128)S(1)}, u32[]{:S(2)}, u32[]{:S(2)}) collective-permute-start(f32[2,128,384]{2,1,0:T(8,128)S(1)} %get-tuple-element.89), channel_id=1, source_target_pairs={{0,1},{2,3},{1,0},{3,2},{4,5},{6,7},{5,4},{7,6},{8,9},{10,11},{9,8... | collective-permute-start | bytes 1179656 | tf_op jit(solution)/shard_map/ppermute | solution.py:34
  87.6 24.9 %collective-permute-start.11 = (f32[2,128,384]{2,1,0:T(8,128)S(1)}, f32[2,128,384]{2,1,0:T(8,128)S(1)}, u32[]{:S(2)}, u32[]{:S(2)}) collective-permute-start(f32[2,128,384]{2,1,0:T(8,128)S(1)} %get-tuple-element.88), channel_id=1, source_target_pairs={{1,2},{2,1},{5,6},{6,5},{9,10},{10,9},{13,14},{14,13},{17,18},{18,... | collective-permute-start | bytes 1179656 | tf_op jit(solution)/shard_map/ppermute | solution.py:34
  90.2 7.4 %collective-permute-start.17 = (f32[128,256]{1,0:T(8,128)S(1)}, f32[128,256]{1,0:T(8,128)S(1)}, u32[]{:S(2)}, u32[]{:S(2)}) collective-permute-start(f32[128,256]{1,0:T(8,128)S(1)} %maximum_select_fusion.3), channel_id=1, source_target_pairs={{0,1},{1,0},{2,3},{3,2},{4,5},{5,4},{6,7},{7,6},{8,9},{9,8},{10,11... | collective-permute-start | bytes 393224 | tf_op jit(solution)/shard_map/ppermute | solution.py:39
  97.6 13.1 %collective-permute-start.18 = (f32[256,256]{1,0:T(8,128)S(1)}, f32[256,256]{1,0:T(8,128)S(1)}, u32[]{:S(2)}, u32[]{:S(2)}) collective-permute-start(f32[256,256]{1,0:T(8,128)S(1)} %maximum_select_fusion.2), channel_id=1, source_target_pairs={{0,8},{4,12},{8,0},{12,4},{1,9},{5,13},{9,1},{13,5},{2,10},{6,14},... | collective-permute-start | bytes 786440 | tf_op jit(solution)/shard_map/ppermute | solution.py:39
  110.7 3.2 %collective-permute-start.19 = (f32[512,256]{1,0:T(8,128)S(1)}, f32[512,256]{1,0:T(8,128)S(1)}, u32[]{:S(2)}, u32[]{:S(2)}) collective-permute-start(f32[512,256]{1,0:T(8,128)S(1)} %maximum_select_fusion.1), channel_id=1, source_target_pairs={{0,4},{4,0},{8,12},{12,8},{1,5},{5,1},{9,13},{13,9},{2,6},{6,2},{1... | collective-permute-start | bytes 1572872 | tf_op jit(solution)/shard_map/ppermute | solution.py:39
  112.8 2.9 %copy-start.5 = (f32[2,384,384]{2,1,0:T(8,128)}, f32[2,384,384]{2,1,0:T(8,128)S(1)}, u32[]{:S(2)}) copy-start(f32[2,384,384]{2,1,0:T(8,128)S(1)} %fusion.2) | copy-start | bytes 3538948

commit v2 on v0

v2 whole, which is shorter than its diff:
```python
import functools
import math

import jax
import jax.numpy as jnp
import ml_dtypes
import numpy as np
from jax import lax
from jax.experimental import pallas as pl
from jax.experimental.pallas import tpu as pltpu
from jax.sharding import PartitionSpec as P

W = 256
MODES = 2
KMAX = 8
HALF = W // 2
LANES = 128
GROUPS = W // 8
VMEM_BYTES = 50 * 1024 * 1024


def tables():
    counter = np.arange(W)
    phases = (counter[:, None] * counter[None, :] % W).astype(np.float32)
    angles = (np.float32(2.0 * math.pi / W) * phases).astype(np.float32)
    scaling = np.float32(1.0 / math.sqrt(W))
    cosine = (np.cos(angles) * scaling).astype(ml_dtypes.bfloat16)
    sine = (np.sin(angles) * scaling).astype(ml_dtypes.bfloat16)
    ahead = np.block([[cosine, -sine], [sine, cosine]])
    back = np.block([[cosine, sine], [-sine, cosine]])
    return ahead, back


def side_pairs(size, parity):
    pairs = [(i, i + 1) for i in range(parity, size - 1, 2)]
    return pairs + [(j, i) for i, j in pairs]


def swap(x, axis, parity):
    return lax.ppermute(x, axis, side_pairs(lax.axis_size(axis), parity))


def exchange(x, axis, bits):
    size = lax.axis_size(axis)
    return lax.ppermute(x, axis, [(i, i ^ bits) for i in range(size)])


def edges(side_ref, tile):
    far_edge = tile + HALF
    row_odd, col_odd = side_ref[0], side_ref[1]
    row_a = pl.multiple_of((1 - row_odd) * far_edge, LANES)
    row_b = pl.multiple_of(row_odd * far_edge, LANES)
    col_a = pl.multiple_of((1 - col_odd) * far_edge, LANES)
    col_b = pl.multiple_of(col_odd * far_edge, LANES)
    return [pl.ds(start, HALF) for start in (row_a, row_b, col_a, col_b)]


def inner_edges(side_ref, tile):
    edge = tile - HALF
    row_odd, col_odd = side_ref[0], side_ref[1]
    row_a = pl.multiple_of((1 - row_odd) * edge, LANES)
    row_b = pl.multiple_of(row_odd * edge, LANES)
    col_a = pl.multiple_of((1 - col_odd) * edge, LANES)
    col_b = pl.multiple_of(col_odd * edge, LANES)
    return [pl.ds(start, HALF) for start in (row_a, row_b, col_a, col_b)]


def run_copies(moves, sems):
    copies = [
        pltpu.make_async_copy(source, target, sems.at[index])
        for index, (source, target) in enumerate(moves)
    ]
    for copy in copies:
        copy.start()
    return copies


def merge(first, second):
    order = [((i + 0.5) / len(first), 0, step) for i, step in enumerate(first)]
    order += [((i + 0.5) / len(second), 1, step) for i, step in enumerate(second)]
    for _, _, step in sorted(order, key=lambda entry: entry[:2]):
        step()


def slots_kernel(
    pieces,
    side_ref,
    offsets_ref,
    count_ref,
    own_ref,
    row_a_ref,
    row_b_ref,
    col_a_ref,
    col_b_ref,
    corner_a_ref,
    corner_b_ref,
    probe_in,
    patterns_in,
    ahead_in,
    back_in,
    probe_keep,
    probe_away,
    inner_out,
    row_a_out,
    row_b_out,
    col_a_out,
    col_b_out,
    corner_out,
    padded,
    grad,
    probe_grad,
    windows,
    *rest,
):
    sets = (rest[0:6], rest[6:12])
    probe_ref, patterns_ref, ahead_ref, back_ref, counted, sems = rest[12:]
    tile = own_ref.shape[1]
    row_a, row_b, col_a, col_b = edges(side_ref, tile)
    middle = pl.ds(HALF, tile)
    copies = run_copies(
        [
            (own_ref, padded.at[:, middle, middle]),
            (row_a_ref, padded.at[:, row_a, middle]),
            (row_b_ref, padded.at[:, row_b, middle]),
            (col_a_ref, padded.at[:, middle, col_a]),
            (col_b_ref, padded.at[:, middle, col_b]),
            (corner_a_ref.at[0], padded.at[:, row_a, col_a]),
            (corner_a_ref.at[1], padded.at[:, row_b, col_a]),
            (corner_b_ref.at[0], padded.at[:, row_a, col_b]),
            (corner_b_ref.at[1], padded.at[:, row_b, col_b]),
            (probe_in, probe_ref),
            (patterns_in, patterns_ref),
            (ahead_in, ahead_ref),
            (back_in, back_ref),
        ],
        sems,
    )
    grad[...] = jnp.zeros_like(grad)
    probe_grad[...] = jnp.zeros_like(probe_grad)
    for buffers in sets:
        buffers[5][...] = jnp.zeros_like(buffers[5])
    for index in (2, 3):
        windows[index] = jnp.zeros(windows.shape[1:], jnp.float32)
    for copy in copies:
        copy.wait()
    lane = lax.broadcasted_iota(jnp.int32, (8, LANES), 1)
    sub = lax.broadcasted_iota(jnp.int32, (8, LANES), 0)
    zero = jnp.zeros((8, LANES), jnp.float32)
    batch = 4
    step = 8 * batch

    def place(k):
        row, column = offsets_ref[0, k], offsets_ref[1, k]
        row_base = pl.multiple_of(row // 8 * 8, 8)
        col_base = pl.multiple_of(column // LANES * LANES, LANES)
        return row_base, row - row_base, col_base, column - col_base

    def make_wave(k, buffers, w):
        wave = buffers[0]
        row_base, row_shift, col_base, col_shift = place(k)
        in_lane, in_sub = lane < LANES - col_shift, sub < 8 - row_shift
        lane_turn = lax.rem(LANES - col_shift, LANES)
        sub_turn = lax.rem(8 - row_shift, 8)
        before = {}

        def turned(plane, group):
            rows = pl.ds(row_base + 8 * group, 8)
            parts = [
                pltpu.roll(padded[plane, rows, pl.ds(col_base + LANES * j, LANES)], lane_turn, 1)
                for j in range(3)
            ]
            return [
                pltpu.roll(jnp.where(in_lane, parts[j], parts[j + 1]), sub_turn, 0)
                for j in range(2)
            ]

        def some_rows(first):
            if first == 0:
                for plane in range(2):
                    before[plane] = turned(plane, 0)
            pieces = [[], []]
            for group in range(first, first + batch):
                for plane in range(2):
                    after = turned(plane, group + 1)
                    value = jnp.concatenate(
                        [jnp.where(in_sub, b, a) for b, a in zip(before[plane], after)], axis=1
                    )
                    windows[w, plane, 8 * group : 8 * group + 8, :] = value
                    pieces[plane].append(value)
                    before[plane] = after
            object_real, object_imag = [jnp.concatenate(piece, axis=0) for piece in pieces]
            start = 8 * first
            rows = slice(start, start + step)
            for m in range(MODES):
                probe_real, probe_imag = probe_ref[0, m, rows, :], probe_ref[1, m, rows, :]
                into = slice(m * W + start, m * W + start + step)
                wave[into, :W] = (probe_real * object_real - probe_imag * object_imag).astype(
                    jnp.bfloat16
                )
                wave[into, W:] = (probe_real * object_imag + probe_imag * object_real).astype(
                    jnp.bfloat16
                )

        return [functools.partial(some_rows, first) for first in range(0, GROUPS, batch)]

    def right(source, table, target, m):
        rows = slice(m * W, m * W + W)
        product = jnp.dot(
            source[rows, :], table[...], preferred_element_type=jnp.float32
        ).astype(jnp.bfloat16)
        target[:W, rows] = product[:, :W]
        target[W:, rows] = product[:, W:]

    def left(source, table, target, m):
        columns = slice(m * W, m * W + W)
        target[:, columns] = jnp.dot(
            table[...], source[:, columns], preferred_element_type=jnp.float32
        )

    def ahead_right(buffers, m):
        return functools.partial(right, buffers[0], ahead_ref, buffers[1], m)

    def ahead_left(buffers, m):
        return functools.partial(left, buffers[1], back_ref, buffers[2], m)

    def back_right(buffers, m):
        return functools.partial(right, buffers[3], back_ref, buffers[4], m)

    def back_left(buffers, m):
        return functools.partial(left, buffers[4], ahead_ref, buffers[5], m)

    def weigh(k, live, buffers):
        far, weighted = buffers[2], buffers[3]

        def some_rows(start):
            rows = slice(start, start + step)
            imag_rows = slice(W + start, W + start + step)
            reals = [far[rows, m * W : m * W + W] for m in range(MODES)]
            imags = [far[imag_rows, m * W : m * W + W] for m in range(MODES)]
            intensity = sum(r * r + i * i for r, i in zip(reals, imags))
            residual = intensity - patterns_ref[k, rows, :].astype(jnp.float32)
            if live is not None:
                residual = residual * live
            for m in range(MODES):
                into = slice(m * W + start, m * W + start + step)
                weighted[into, :W] = (residual * reals[m]).astype(jnp.bfloat16)
                weighted[into, W:] = (residual * imags[m]).astype(jnp.bfloat16)

        return [functools.partial(some_rows, start) for start in range(0, W, step)]

    def add_terms(members):
        info = []
        for k, _, _ in members:
            row_base, row_shift, col_base, col_shift = place(k)
            info.append(
                (row_base, row_shift, col_base, col_shift, lane >= col_shift, sub >= row_shift)
            )

        def terms(start, low):
            rows = slice(start, start + 8)
            imag_rows = slice(W + start, W + start + 8)
            columns = slice(low, low + LANES)
            turned = []
            totals = [[None, None] for _ in range(MODES)]
            probes = [[probe_ref[plane, m, rows, columns] for plane in range(2)] for m in range(MODES)]
            for (_, buffers, w), (_, row_shift, _, col_shift, _, _) in zip(members, info):
                chi = buffers[5]
                object_real, object_imag = windows[w, 0, rows, columns], windows[w, 1, rows, columns]
                sums = [None, None]
                for m in range(MODES):
                    at = slice(m * W + low, m * W + low + LANES)
                    chi_real, chi_imag = chi[rows, at], chi[imag_rows, at]
                    probe_real, probe_imag = probes[m]
                    mine = (
                        object_real * chi_real + object_imag * chi_imag,
                        object_real * chi_imag - object_imag * chi_real,
                    )
                    more = (
                        probe_real * chi_real + probe_imag * chi_imag,
                        probe_real * chi_imag - probe_imag * chi_real,
                    )
                    for plane in range(2):
                        total = totals[m][plane]
                        totals[m][plane] = mine[plane] if total is None else total + mine[plane]
                        total = sums[plane]
                        sums[plane] = more[plane] if total is None else total + more[plane]
                turned.append(
                    [pltpu.roll(pltpu.roll(value, col_shift, 1), row_shift, 0) for value in sums]
                )
            for m in range(MODES):
                for plane in range(2):
                    probe_grad[plane, m, rows, columns] += totals[m][plane]
            return turned

        nothing = [[zero, zero] for _ in members]
        before = [nothing, nothing]

        def some_groups(first):
            groups = range(first, min(first + batch, GROUPS + 1))
            news = []
            for group in groups:
                if group < GROUPS:
                    news.append([terms(8 * group, 0), terms(8 * group, LANES)])
                else:
                    news.append([nothing, nothing])
            for q, (row_base, _, col_base, _, from_lane, from_sub) in enumerate(info):
                adds = []
                last = [before[0][q], before[1][q]]
                for group, new in zip(groups, news):
                    rows = pl.ds(row_base + 8 * group, 8)
                    for plane in range(2):
                        low, high = [
                            jnp.where(from_sub, new[half][q][plane], last[half][plane])
                            for half in range(2)
                        ]
                        values = (
                            jnp.where(from_lane, low, 0.0),
                            jnp.where(from_lane, high, low),
                            jnp.where(from_lane, 0.0, high),
                        )
                        for j, value in enumerate(values):
                            adds.append((plane, rows, pl.ds(col_base + LANES * j, LANES), value))
                    last = [new[0][q], new[1][q]]
                olds = [grad[plane, rows, columns] for plane, rows, columns, _ in adds]
                for (plane, rows, columns, value), old in zip(adds, olds):
                    grad[plane, rows, columns] = old + value
            before[:] = news[-1]

        return [functools.partial(some_groups, first) for first in range(0, GROUPS + 1, batch)]

    count = count_ref[0]
    pairs = (count + 1) // 2
    x, y = sets
    for each in make_wave(0, x, 0) + make_wave(1, y, 1):
        each()

    def pair(index, carry):
        now = (2 * index, 2 * index + 1)
        past = [jnp.maximum(k - 2, 0) for k in now]
        later = [jnp.minimum(k + 2, KMAX - 1) for k in now]
        other = 2 - lax.rem(index, 2) * 2
        live = (now[1] < count).astype(jnp.float32)
        adds = add_terms([(past[0], x, other), (past[1], y, other + 1)])
        some = len(adds) * 2 // 3
        merge(
            [ahead_right(b, m) for b in sets for m in range(MODES)]
            + [ahead_left(x, m) for m in range(MODES)],
            adds[:some],
        )
        merge([ahead_left(y, m) for m in range(MODES)], adds[some:] + weigh(now[0], None, x))
        merge([back_right(x, m) for m in range(MODES)], weigh(now[1], live, y))
        merge(
            [back_right(y, m) for m in range(MODES)]
            + [back_left(b, m) for b in sets for m in range(MODES)],
            make_wave(later[0], x, other) + make_wave(later[1], y, other + 1),
        )
        return carry

    lax.fori_loop(0, pairs, pair, 0)
    final = pairs - 1
    at = lax.rem(final, 2) * 2
    for each in add_terms([(2 * final, x, at), (2 * final + 1, y, at + 1)]):
        each()

    moves = [
        (grad.at[:, middle, middle], inner_out),
        (grad.at[:, row_a, middle], row_a_out.at[:, :, pl.ds(0, tile)]),
        (grad.at[:, row_b, middle], row_b_out.at[:, :, pl.ds(0, tile)]),
        (grad.at[:, row_a, col_b], row_a_out.at[:, :, pl.ds(tile, HALF)]),
        (grad.at[:, row_b, col_b], row_b_out.at[:, :, pl.ds(tile, HALF)]),
        (grad.at[:, middle, col_a], col_a_out),
        (grad.at[:, middle, col_b], col_b_out),
        (grad.at[:, row_a, col_a], corner_out.at[0]),
        (grad.at[:, row_b, col_a], corner_out.at[1]),
    ]
    me = side_ref[2]
    half_rows = probe_keep.shape[0] - 8
    height = 2 * half_rows // pieces
    per_square = W // height
    for piece in range(pieces):
        which = piece ^ me
        square, block = which // per_square, lax.rem(which, per_square)
        source = probe_grad.at[
            square // MODES, lax.rem(square, MODES), pl.ds(pl.multiple_of(block * height, 8), height)
        ]
        target = probe_keep if piece < pieces // 2 else probe_away
        moves.append((source, target.at[pl.ds(piece % (pieces // 2) * height, height)]))
    counted[...] = jnp.full(counted.shape, count.astype(jnp.float32))
    moves += [(counted, target.at[pl.ds(half_rows, 8)]) for target in (probe_keep, probe_away)]
    for copy in run_copies(moves, sems):
        copy.wait()


def slots(sides, offsets, count, own, halos, probe, patterns, pieces):
    tile = own.shape[1]
    wide = tile + 2 * HALF
    smem = pl.BlockSpec(memory_space=pltpu.SMEM)
    anywhere = pl.BlockSpec(memory_space=pl.ANY)
    ahead, back = tables()
    square = (2 * W, 2 * W)
    buffers = [
        pltpu.VMEM(square, kind)
        for kind in (jnp.bfloat16, jnp.bfloat16, jnp.float32, jnp.bfloat16, jnp.bfloat16, jnp.float32)
    ]
    outs = [
        (MODES * W + 8, W),
        (MODES * W + 8, W),
        (2, tile, tile),
        (2, HALF, tile + HALF),
        (2, HALF, tile + HALF),
        (2, tile, HALF),
        (2, tile, HALF),
        (2, 2, HALF, HALF),
    ]
    return pl.pallas_call(
        functools.partial(slots_kernel, pieces),
        out_shape=[jax.ShapeDtypeStruct(shape, jnp.float32) for shape in outs],
        in_specs=[smem] * 3 + [pl.BlockSpec(memory_space=pltpu.HBM)] * 11,
        out_specs=[anywhere] * len(outs),
        scratch_shapes=[
            pltpu.VMEM((2, wide, wide), jnp.float32),
            pltpu.VMEM((2, wide, wide), jnp.float32),
            pltpu.VMEM((2, MODES, W, W), jnp.float32),
            pltpu.VMEM((4, 2, W, W), jnp.float32),
            *buffers,
            *buffers,
            pltpu.VMEM(probe.shape, jnp.float32),
            pltpu.VMEM(patterns.shape, patterns.dtype),
            pltpu.VMEM(square, jnp.bfloat16),
            pltpu.VMEM(square, jnp.bfloat16),
            pltpu.VMEM((8, W), jnp.float32),
            pltpu.SemaphoreType.DMA((13 + pieces,)),
        ],
        compiler_params=pltpu.CompilerParams(vmem_limit_bytes=VMEM_BYTES),
    )(sides, offsets, count, own, *halos, probe, patterns, jnp.asarray(ahead), jnp.asarray(back))


def join_kernel(
    side_ref, inner_ref, row_a_ref, row_b_ref, col_a_ref, col_b_ref, out_ref
):
    row_a, row_b, col_a, col_b = inner_edges(side_ref, inner_ref.shape[1])
    out_ref[...] = inner_ref[...]
    out_ref[:, row_a, :] += row_a_ref[...]
    out_ref[:, row_b, :] += row_b_ref[...]
    out_ref[:, :, col_a] += col_a_ref[...]
    out_ref[:, :, col_b] += col_b_ref[...]


def join(sides, inner, *terms):
    vmem = pl.BlockSpec(memory_space=pltpu.VMEM)
    return pl.pallas_call(
        join_kernel,
        out_shape=jax.ShapeDtypeStruct(inner.shape, jnp.float32),
        in_specs=[pl.BlockSpec(memory_space=pltpu.SMEM)] + [vmem] * (1 + len(terms)),
        out_specs=vmem,
        compiler_params=pltpu.CompilerParams(vmem_limit_bytes=VMEM_BYTES),
    )(sides, inner, *terms)


def cut(x, start, dim):
    return lax.dynamic_slice_in_dim(x, start, HALF, axis=dim)


def add_at(strip, term, start):
    old = lax.dynamic_slice_in_dim(strip, start, term.shape[2], axis=2)
    return lax.dynamic_update_slice_in_dim(strip, old + term, start, axis=2)


def gathered(part, axis, bits):
    other = exchange(part, axis, bits)
    first = lax.axis_index(axis) // bits % 2 == 0
    return jnp.where(first, jnp.concatenate([part, other]), jnp.concatenate([other, part]))


def local(object_field, probe, positions, counts, patterns):
    tile = object_field.shape[1]
    edge = tile - HALF
    barrier = lax.optimization_barrier
    row, col = lax.axis_index("row"), lax.axis_index("col")
    live = counts[0, 0]
    halvings = [
        (axis, 1 << i)
        for axis in ("col", "row")
        for i in range(lax.axis_size(axis).bit_length() - 1)
    ]
    halvings, last = halvings[:-1], halvings[-1]
    pieces = 1 << len(halvings)
    mine = 0
    for axis, bits in halvings:
        mine = 2 * mine + lax.axis_index(axis) // bits % 2
    sides = jnp.stack([row % 2, col % 2, mine]).astype(jnp.int32)

    row_a = swap(cut(object_field, (1 - row % 2) * edge, 1), "row", 0)
    row_b = swap(cut(object_field, row % 2 * edge, 1), "row", 1)
    col_a = swap(cut(object_field, (1 - col % 2) * edge, 2), "col", 0)
    col_b = swap(cut(object_field, col % 2 * edge, 2), "col", 1)
    corner_a = jnp.stack([cut(strip, (1 - col % 2) * edge, 2) for strip in (row_a, row_b)])
    corner_b = jnp.stack([cut(strip, col % 2 * edge, 2) for strip in (row_a, row_b)])
    corner_b = swap(corner_b, "col", 1)
    corner_a = swap(corner_a, "col", 0)

    keep, away, inner, row_a, row_b, col_a, col_b, corner = slots(
        sides,
        positions[0, 0],
        live[None],
        object_field,
        (row_a, row_b, col_a, col_b, corner_a, corner_b),
        probe,
        patterns[0, 0],
        pieces,
    )

    corner = swap(corner, "col", 0)
    away = exchange(away, *halvings[0])
    row_a = swap(add_at(row_a, corner[0], (1 - col % 2) * edge), "row", 0)
    row_b = swap(add_at(row_b, corner[1], (1 - col % 2) * edge), "row", 1)
    keep = keep + away
    col_a = swap(col_a, "col", 0)
    for index, (axis, bits) in enumerate(halvings[1:]):
        half = (keep.shape[0] - 8) // 2
        keep = jnp.concatenate([keep[:half], keep[-8:]]) + exchange(keep[half:], axis, bits)
        if index == 0:
            keep, row_a, row_b, col_a, col_b = barrier((keep, row_a, row_b, col_a, col_b))
            top, bottom = [
                jnp.where(row % 2 == 1, first, second)[:, :, tile:]
                for first, second in ((row_a, row_b), (row_b, row_a))
            ]
            blank = jnp.zeros((2, tile - 2 * HALF, HALF), jnp.float32)
            col_b = swap(col_b + jnp.concatenate([top, blank, bottom], axis=1), "col", 1)
    keep = keep + exchange(keep, *last)
    part = keep[:-8] / keep[-8:-7]
    for axis, bits in reversed(halvings):
        if bits == 1 and axis == "row":
            part = gathered(part, axis, bits)
            part, col_b = barrier((part, col_b))
        elif (axis, bits) != halvings[0]:
            part = gathered(part, axis, bits)
    result = join(sides, inner, row_a[:, :, :tile], row_b[:, :, :tile], col_a, col_b)
    part, result = barrier((part, result))
    whole = gathered(part, *halvings[0])
    return result, whole.reshape(probe.shape)


def solution(mesh):
    placed = (
        P(None, ("groups", "row"), "col"),
        P(None, "groups", None, None),
        P(("groups", "row"), "col", None, None),
        P(("groups", "row"), "col"),
        P(("groups", "row"), "col", None, None, None),
    )
    return jax.shard_map(
        local,
        mesh=mesh,
        in_specs=placed,
        out_specs=(P(None, ("groups", "row"), "col"), P(None, "groups", None, None)),
        check_vma=False,
    )
```

time: 387 us -> 91.3 us (0.24); the launches traced: 381 us -> 91.5 us
  local copies, waits for them, and re-layouts: 91.9 us -> 4.26 us
  other arithmetic: 82.2 us -> 6.82 us
  blocking collectives: 42.6 us -> 0 us
  waiting for transfers between devices: 66.9 us -> 30.7 us
  matrix products: 32 us -> 0 us
  loops' own time: 30.3 us -> 0 us
  starting transfers between devices: 20.4 us -> 37 us
  between operations: 14.9 us -> 1.64 us
  Pallas kernels: 0 us -> 11.1 us
    dynamic_update_slice x8 -> x0, local copies, waits for them, and re-layouts: 51.9 us -> none  [one_block(): lax.dynamic_update_slice(gradient, current + object_terms[slot_index], co...]
    psum x1 -> x0, waiting for transfers between devices: 43.9 us -> none  [local(): lax.psum((probe_total, count_here), ('col', 'row'))]
    psum x1 -> x0, blocking collectives: 42.6 us -> none  [local(): lax.psum((probe_total, count_here), ('col', 'row'))]
    dot_general x24 -> x0, matrix products: 32 us -> none  [the longest x8 11.2 us: transform(): jnp.einsum('jk,bkx->bjx', sine_table, halfway, preferred_element_type=jnp...]
    another operation x1 -> x0, loops' own time: 30.3 us -> none  [local(): gradient, probe_total = lax.fori_loop(0, block_count, one_block, start)]
    add x16 -> x5, other arithmetic: 26.3 us -> 2.25 us  [the longest x1 1.11 us: local(): keep = keep + away]
    ppermute x8 -> x18, starting transfers between devices: 20.3 us -> 37 us  [the longest x11 30.4 us: swap(): return lax.ppermute(x, axis, side_pairs(lax.axis_size(axis), parity))]
    reduce_sum x8 -> x0, other arithmetic: 14.8 us -> none  [the longest x4 13.5 us: one_block(): jnp.sum(object_real * back_real + object_imag * back_imag, axis=0)]
  transfers between devices with their start and end apart: 9 -> 18, of which waited for: 7 -> 10; matrix products, arithmetic and copies ran while one was open for 3% -> 9% of each run, Pallas kernels for 0% -> 2%
where the time goes in v2:
time: 91.3 us; the launch traced here: 91.5 us
  starting transfers between devices  37 us (41%)
  waiting for transfers between devices  30.7 us (34%)
  Pallas kernels  11.1 us (12%)
  other arithmetic  6.82 us (7%)
  local copies, waits for them, and re-layouts  4.26 us (5%)
  between operations  1.64 us (2%)
    ppermute x11, starting transfers between devices, swap(): return lax.ppermute(x, axis, side_pairs(lax.axis_size(axis), parity))  30.4 us
    ppermute x7, waiting for transfers between devices, exchange(): return lax.ppermute(x, axis, [(i, i ^ bits) for i in range(size)])  18.1 us
    ppermute x11, waiting for transfers between devices, swap(): return lax.ppermute(x, axis, side_pairs(lax.axis_size(axis), parity))  12.6 us
    pallas_call x1, Pallas kernels, slots(): pl.pallas_call(functools.partial(slots_kernel, pieces), out_shape=[jax.Sh...  9.29 us
    ppermute x7, starting transfers between devices, exchange(): return lax.ppermute(x, axis, [(i, i ^ bits) for i in range(size)])  6.6 us
    dynamic_slice x2, local copies, waits for them, and re-layouts, cut(): return lax.dynamic_slice_in_dim(x, start, HALF, axis=dim)  2.08 us
  transfers between devices with their start and end apart: 18, of which 10 were waited for; matrix products, arithmetic and copies ran while one was open for 9% of the time, Pallas kernels for 2%

profile of v2, /device:TPU:5, one launch (start us, length us, event | category | flops | bytes accessed | tf_op | source)
XLA Modules:
  0.0 91.5 jit_solution(9797667777499008787)
XLA Ops:
  0.6 0.0 copy-start.2
  0.7 2.0 %constant_dynamic-slice_fusion.2 = (f32[2,128,384]{2,1,0:T(8,128)S(1)}, f32[2,128,384]{2,1,0:T(8,128)}) fusion(f32[2,384,384]{2,1,0:T(8,128)} %own_ref.1, s32[]{:T(128)S(6)} %select_n.127, s32[]{:T(128)S(6)} %select_n.126), kind=kLoop, calls=%fused_computation.23 | loop fusion | bytes 1572872 | tf_op jit(solution)/shard_map/dynamic_slice | solution.py:461
  2.7 1.3 %collective-permute-start = (f32[2,128,384]{2,1,0:T(8,128)}, f32[2,128,384]{2,1,0:T(8,128)S(1)}, u32[]{:S(2)}, u32[]{:S(2)}) collective-permute-start(f32[2,128,384]{2,1,0:T(8,128)} %get-tuple-element.39), channel_id=1, source_target_pairs={{0,1},{2,3},{1,0},{3,2},{4,5},{6,7},{5,4},{7,6},{8,9},{10,11},{9,8... | collective-permute-start | bytes 1179656 | tf_op jit(solution)/shard_map/ppermute | solution.py:40
  4.0 0.7 collective-permute-start.1
  4.7 0.1 constant_dynamic-slice_fusion
  4.8 0.0 copy-start.1
  4.8 1.0 %collective-permute-start.2 = (f32[2,384,128]{2,1,0:T(8,128)S(1)}, f32[2,384,128]{2,1,0:T(8,128)S(1)}, u32[]{:S(2)}, u32[]{:S(2)}) collective-permute-start(f32[2,384,128]{2,1,0:T(8,128)S(1)} %get-tuple-element.37), channel_id=1, source_target_pairs={{0,4},{8,12},{4,0},{12,8},{1,5},{9,13},{5,1},{13,9},{2,6},{10,14},... | collective-permute-start | bytes 1179656 | tf_op jit(solution)/shard_map/ppermute | solution.py:40
  5.8 3.0 %collective-permute-start.3 = (f32[2,384,128]{2,1,0:T(8,128)S(1)}, f32[2,384,128]{2,1,0:T(8,128)S(1)}, u32[]{:S(2)}, u32[]{:S(2)}) collective-permute-start(f32[2,384,128]{2,1,0:T(8,128)S(1)} %get-tuple-element.36), channel_id=1, source_target_pairs={{4,8},{8,4},{5,9},{9,5},{6,10},{10,6},{7,11},{11,7},{20,24},{24,20... | collective-permute-start | bytes 1179656 | tf_op jit(solution)/shard_map/ppermute | solution.py:40
  8.8 4.1 %collective-permute-done.row_a_ref = f32[2,128,384]{2,1,0:T(8,128)S(1)} collective-permute-done((f32[2,128,384]{2,1,0:T(8,128)}, f32[2,128,384]{2,1,0:T(8,128)S(1)}, u32[]{:S(2)}, u32[]{:S(2)}) %collective-permute-start) | collective-permute-done | bytes 393248 | tf_op jit(solution)/shard_map/ppermute | solution.py:40
  13.0 1.6 %collective-permute-start.4 = (f32[2,2,128,128]{3,2,1,0:T(8,128)S(1)}, f32[2,2,128,128]{3,2,1,0:T(8,128)S(1)}, u32[]{:S(2)}, u32[]{:S(2)}) collective-permute-start(f32[2,2,128,128]{3,2,1,0:T(8,128)S(1)} %pad_maximum_fusion), channel_id=1, source_target_pairs={{0,4},{8,12},{4,0},{12,8},{1,5},{9,13},{5,1},{13,9},{2,6},{10,14},... | collective-permute-start | bytes 786440 | tf_op jit(solution)/shard_map/ppermute | solution.py:40
  14.6 0.7 pad_maximum_fusion.1
  15.3 3.0 %collective-permute-start.5 = (f32[2,2,128,128]{3,2,1,0:T(8,128)}, f32[2,2,128,128]{3,2,1,0:T(8,128)S(1)}, u32[]{:S(2)}, u32[]{:S(2)}) collective-permute-start(f32[2,2,128,128]{3,2,1,0:T(8,128)} %pad_maximum_fusion.1), channel_id=1, source_target_pairs={{4,8},{8,4},{5,9},{9,5},{6,10},{10,6},{7,11},{11,7},{20,24},{24,20... | collective-permute-start | bytes 786440 | tf_op jit(solution)/shard_map/ppermute | solution.py:40
  19.0 0.1 pad_add_fusion.side_ref
  19.1 0.0 collective-permute-done.2.col_a_ref
  19.1 0.0 collective-permute-done.3.col_b_ref
  19.1 0.0 collective-permute-done.4.corner_a_ref
  19.1 4.1 %collective-permute-done.5.corner_b_ref = f32[2,2,128,128]{3,2,1,0:T(8,128)S(1)} collective-permute-done((f32[2,2,128,128]{3,2,1,0:T(8,128)}, f32[2,2,128,128]{3,2,1,0:T(8,128)S(1)}, u32[]{:S(2)}, u32[]{:S(2)}) %collective-permute-start.5) | collective-permute-done | bytes 262176 | tf_op jit(solution)/shard_map/ppermute | solution.py:40
  23.2 9.3 %shard_map.86 = (f32[520,256]{1,0:T(8,128)}, f32[520,256]{1,0:T(8,128)}, f32[2,384,384]{2,1,0:T(8,128)}, f32[2,128,512]{2,1,0:T(8,128)S(1)}, f32[2,128,512]{2,1,...) custom-call(s32[3]{0:T(128)S(1)} %pad_add_fusion.side_ref, ...), custom_call_target="tpu_custom_call" | custom-call | tf_op jit(solution)/shard_map/pallas_call | solution.py:415
  32.5 0.1 collective-permute-start.6
  32.6 0.5 collective-permute-start.8
  33.1 2.0 %collective-permute-done.8 = f32[2,2,128,128]{3,2,1,0:T(8,128)S(1)} collective-permute-done((f32[2,2,128,128]{3,2,1,0:T(8,128)}, f32[2,2,128,128]{3,2,1,0:T(8,128)S(1)}, u32[]{:S(2)}, u32[]{:S(2)}) %collective-permute-start.8) | collective-permute-done | bytes 262176 | tf_op jit(solution)/shard_map/ppermute | solution.py:40
  35.1 1.6 %fusion.1 = (f32[2,128,512]{2,1,0:T(8,128)}, f32[2,128,512]{2,1,0:T(8,128)S(1)}) fusion(f32[2,128,512]{2,1,0:T(8,128)} %get-tuple-element.23, s32[]{:T(128)S(6)} %select_n.130, f32[2,2,128,128]{3,2,1,0:T(8,128)S(1)} %collective-permute-done.8, f32[2,128,512]{2,1,0:T(8,128)S(1)} %get-tuple-element.21), kind=kLoop, calls=%fused_computation.11 | loop fusion | flops 65536 | bytes 786436 | tf_op jit(solution)/shard_map/dynamic_update_slice | solution.py:466
  36.7 1.5 %collective-permute-start.10 = (f32[2,128,512]{2,1,0:T(8,128)}, f32[2,128,512]{2,1,0:T(8,128)}, u32[]{:S(2)}, u32[]{:S(2)}) collective-permute-start(f32[2,128,512]{2,1,0:T(8,128)} %get-tuple-element.46), channel_id=1, source_target_pairs={{1,2},{2,1},{5,6},{6,5},{9,10},{10,9},{13,14},{14,13},{17,18},{18,... | collective-permute-start | bytes 1572872 | tf_op jit(solution)/shard_map/ppermute | solution.py:40
  38.2 12.6 %collective-permute-start.9 = (f32[2,128,512]{2,1,0:T(8,128)S(1)}, f32[2,128,512]{2,1,0:T(8,128)}, u32[]{:S(2)}, u32[]{:S(2)}) collective-permute-start(f32[2,128,512]{2,1,0:T(8,128)S(1)} %get-tuple-element.47), channel_id=1, source_target_pairs={{0,1},{2,3},{1,0},{3,2},{4,5},{6,7},{5,4},{7,6},{8,9},{10,11},{9,8... | collective-permute-start | bytes 1572872 | tf_op jit(solution)/shard_map/ppermute | solution.py:40
  50.7 1.1 %add.88 = f32[520,256]{1,0:T(8,128)S(1)} add(f32[520,256]{1,0:T(8,128)} %get-tuple-element.19, f32[520,256]{1,0:T(8,128)S(1)} %collective-permute-done.6) | non-fusion elementwise | flops 133120 | bytes 1597440 | tf_op jit(solution)/shard_map/add | solution.py:517
  51.9 0.1 collective-permute-start.7
  52.0 0.8 collective-permute-start.11
  52.8 6.6 %collective-permute-done.7 = f32[264,256]{1,0:T(8,128)} collective-permute-done((f32[264,256]{1,0:T(8,128)S(1)}, f32[264,256]{1,0:T(8,128)}, u32[]{:S(2)}, u32[]{:S(2)}) %collective-permute-start.7) | collective-permute-done | bytes 270368 | tf_op jit(solution)/shard_map/ppermute | solution.py:45
  59.4 1.0 %maximum_add_fusion.1 = f32[264,256]{1,0:T(8,128)S(1)} fusion(f32[264,256]{1,0:T(8,128)} %collective-permute-done.7, f32[8,256]{1,0:T(8,128)S(1)} %slice.57, f32[256,256]{1,0:T(8,128)S(1)} %slice.56), kind=kLoop, calls=%fused_computation.3 | loop fusion | flops 135168 | bytes 811008 | tf_op jit(solution)/shard_map/add | solution.py:521
  60.4 2.4 %collective-permute-done.9 = f32[2,128,512]{2,1,0:T(8,128)} collective-permute-done((f32[2,128,512]{2,1,0:T(8,128)S(1)}, f32[2,128,512]{2,1,0:T(8,128)}, u32[]{:S(2)}, u32[]{:S(2)}) %collective-permute-start.9) | collective-permute-done | bytes 524320 | tf_op jit(solution)/shard_map/ppermute | solution.py:40
  62.8 1.2 %collective-permute-start.12 = (f32[136,256]{1,0:T(8,128)S(1)}, f32[136,256]{1,0:T(8,128)S(1)}, u32[]{:S(2)}, u32[]{:S(2)}) collective-permute-start(f32[136,256]{1,0:T(8,128)S(1)} %slice.49), channel_id=1, source_target_pairs={{0,1},{1,0},{2,3},{3,2},{4,5},{5,4},{6,7},{7,6},{8,9},{9,8},{10,11... | collective-permute-start | bytes 417800 | tf_op jit(solution)/shard_map/ppermute | solution.py:45
  64.0 1.0 %slice_select_fusion.1 = (f32[2,128,128]{2,1,0:T(8,128)S(1)}, f32[2,128,128]{2,1,0:T(8,128)S(1)}) fusion(f32[2,128,512]{2,1,0:T(8,128)} %collective-permute-done.10, f32[2,128,512]{2,1,0:T(8,128)} %collective-permute-done.9, pred[]{:T(512)S(6)} %eq.36), kind=kLoop, calls=%fused_computation.20 | loop fusion | flops 65536 | bytes 524289 | tf_op jit(solution)/shard_map/jit(_where)/select_n | solution.py:525
  65.0 2.1 %collective-permute-done.12 = f32[136,256]{1,0:T(8,128)S(1)} collective-permute-done((f32[136,256]{1,0:T(8,128)S(1)}, f32[136,256]{1,0:T(8,128)S(1)}, u32[]{:S(2)}, u32[]{:S(2)}) %collective-permute-start.12) | collective-permute-done | bytes 139296 | tf_op jit(solution)/shard_map/ppermute | solution.py:45
  67.1 1.4 %collective-permute-start.13 = (f32[136,256]{1,0:T(8,128)S(1)}, f32[136,256]{1,0:T(8,128)S(1)}, u32[]{:S(2)}, u32[]{:S(2)}) collective-permute-start(f32[136,256]{1,0:T(8,128)S(1)} %maximum_add_fusion.2), channel_id=1, source_target_pairs={{0,2},{1,3},{2,0},{3,1},{4,6},{5,7},{6,4},{7,5},{8,10},{9,11},{10,... | collective-permute-start | bytes 417800 | tf_op jit(solution)/shard_map/ppermute | solution.py:45
  68.5 0.1 maximum_add_fusion
  68.6 4.4 %collective-permute-start.15 = (f32[2,384,128]{2,1,0:T(8,128)S(1)}, f32[2,384,128]{2,1,0:T(8,128)S(1)}, u32[]{:S(2)}, u32[]{:S(2)}) collective-permute-start(f32[2,384,128]{2,1,0:T(8,128)S(1)} %maximum_add_fusion), channel_id=1, source_target_pairs={{4,8},{8,4},{5,9},{9,5},{6,10},{10,6},{7,11},{11,7},{20,24},{24,20... | collective-permute-start | bytes 1179656 | tf_op jit(solution)/shard_map/ppermute | solution.py:40
  73.1 2.8 %collective-permute-done.13 = f32[136,256]{1,0:T(8,128)S(1)} collective-permute-done((f32[136,256]{1,0:T(8,128)S(1)}, f32[136,256]{1,0:T(8,128)S(1)}, u32[]{:S(2)}, u32[]{:S(2)}) %collective-permute-start.13) | collective-permute-done | bytes 139296 | tf_op jit(solution)/shard_map/ppermute | solution.py:45
  75.9 0.0 copy-start
  75.9 0.1 collective-permute-start.14
  76.0 3.8 %collective-permute-done.14 = f32[128,256]{1,0:T(8,128)S(1)} collective-permute-done((f32[128,256]{1,0:T(8,128)S(1)}, f32[128,256]{1,0:T(8,128)S(1)}, u32[]{:S(2)}, u32[]{:S(2)}) %collective-permute-start.14) | collective-permute-done | bytes 131104 | tf_op jit(solution)/shard_map/ppermute | solution.py:45
  79.9 0.2 collective-permute-start.16
  80.0 1.0 %slice.54.row_a_ref = f32[2,128,384]{2,1,0:T(8,128)S(1)} slice(f32[2,128,512]{2,1,0:T(8,128)} %collective-permute-done.9), slice={[0:2], [0:128], [0:384]} | slice | bytes 786432 | tf_op jit(solution)/shard_map/slice | solution.py:538
  81.0 1.0 %slice.55.row_b_ref = f32[2,128,384]{2,1,0:T(8,128)S(1)} slice(f32[2,128,512]{2,1,0:T(8,128)} %collective-permute-done.10), slice={[0:2], [0:128], [0:384]} | slice | bytes 786432 | tf_op jit(solution)/shard_map/slice | solution.py:538
  82.1 1.8 %shard_map.87 = f32[2,384,384]{2,1,0:T(8,128)} custom-call(s32[3]{0:T(128)S(1)} %pad_add_fusion.side_ref, f32[2,384,384]{2,1,0:T(8,128)S(1)} %copy-done, f32[2,128,384]{2,1,0:T(8,128)S(1)} %slice.54.row_a_ref, f32[2,128,384]{2,1,0:T(8,128)S(1)} %slice.55.row_b_ref, f32[2,384,128]{2,1,0:T(8,128)S(1)} %collective-permute-done.11.col_a_ref, ...), custom_call_target="tpu_custom_call" | custom-call | tf_op jit(solution)/shard_map/pallas_call | solution.py:451
  83.9 1.3 %collective-permute-done.16 = f32[256,256]{1,0:T(8,128)S(1)} collective-permute-done((f32[256,256]{1,0:T(8,128)S(1)}, f32[256,256]{1,0:T(8,128)S(1)}, u32[]{:S(2)}, u32[]{:S(2)}) %collective-permute-start.16) | collective-permute-done | bytes 262176 | tf_op jit(solution)/shard_map/ppermute | solution.py:45
  85.2 3.7 %collective-permute-start.17 = (f32[512,256]{1,0:T(8,128)S(1)}, f32[512,256]{1,0:T(8,128)S(1)}, u32[]{:S(2)}, u32[]{:S(2)}) collective-permute-start(f32[512,256]{1,0:T(8,128)S(1)} %maximum_select_fusion.1), channel_id=1, source_target_pairs={{0,4},{4,0},{8,12},{12,8},{1,5},{5,1},{9,13},{13,9},{2,6},{6,2},{1... | collective-permute-start | bytes 1572872 | tf_op jit(solution)/shard_map/ppermute | solution.py:45
  88.9 1.5 %collective-permute-done.17 = f32[512,256]{1,0:T(8,128)S(1)} collective-permute-done((f32[512,256]{1,0:T(8,128)S(1)}, f32[512,256]{1,0:T(8,128)S(1)}, u32[]{:S(2)}, u32[]{:S(2)}) %collective-permute-start.17) | collective-permute-done | bytes 524320 | tf_op jit(solution)/shard_map/ppermute | solution.py:45
  90.4 1.1 %maximum_select_fusion = f32[1024,256]{1,0:T(8,128)} fusion(f32[512,256]{1,0:T(8,128)S(1)} %collective-permute-done.17, f32[512,256]{1,0:T(8,128)S(1)} %maximum_select_fusion.1, pred[]{:T(512)S(6)} %eq.37), kind=kLoop, calls=%fused_computation | loop fusion | flops 786432 | bytes 2097153 | tf_op jit(solution)/shard_map/jit(_where)/select_n | solution.py:472
  (25 shorter events, 0.3 us)
Async XLA Ops:
  0.6 4.1 %copy-start.2 = (f32[2,384,384]{2,1,0:T(8,128)S(1)}, f32[2,384,384]{2,1,0:T(8,128)}, u32[]{:S(2)}) copy-start(f32[2,384,384]{2,1,0:T(8,128)} %own_ref.1) | copy-start | bytes 3538948
  2.7 10.2 %collective-permute-start = (f32[2,128,384]{2,1,0:T(8,128)}, f32[2,128,384]{2,1,0:T(8,128)S(1)}, u32[]{:S(2)}, u32[]{:S(2)}) collective-permute-start(f32[2,128,384]{2,1,0:T(8,128)} %get-tuple-element.39), channel_id=1, source_target_pairs={{0,1},{2,3},{1,0},{3,2},{4,5},{6,7},{5,4},{7,6},{8,9},{10,11},{9,8... | collective-permute-start | bytes 1179656 | tf_op jit(solution)/shard_map/ppermute | solution.py:40
  4.0 8.9 %collective-permute-start.1 = (f32[2,128,384]{2,1,0:T(8,128)S(1)}, f32[2,128,384]{2,1,0:T(8,128)S(1)}, u32[]{:S(2)}, u32[]{:S(2)}) collective-permute-start(f32[2,128,384]{2,1,0:T(8,128)S(1)} %get-tuple-element.38), channel_id=1, source_target_pairs={{1,2},{2,1},{5,6},{6,5},{9,10},{10,9},{13,14},{14,13},{17,18},{18,... | collective-permute-start | bytes 1179656 | tf_op jit(solution)/shard_map/ppermute | solution.py:40
  4.8 18.4 %copy-start.1 = (s32[1,1,2,8]{3,2,1,0:T(2,128)S(1)}, s32[1,1,2,8]{3,2,1,0:T(2,128)}, u32[]{:S(2)}) copy-start(s32[1,1,2,8]{3,2,1,0:T(2,128)} %param.9) | copy-start | bytes 196
  4.8 14.3 %collective-permute-start.2 = (f32[2,384,128]{2,1,0:T(8,128)S(1)}, f32[2,384,128]{2,1,0:T(8,128)S(1)}, u32[]{:S(2)}, u32[]{:S(2)}) collective-permute-start(f32[2,384,128]{2,1,0:T(8,128)S(1)} %get-tuple-element.37), channel_id=1, source_target_pairs={{0,4},{8,12},{4,0},{12,8},{1,5},{9,13},{5,1},{13,9},{2,6},{10,14},... | collective-permute-start | bytes 1179656 | tf_op jit(solution)/shard_map/ppermute | solution.py:40
  5.8 13.3 %collective-permute-start.3 = (f32[2,384,128]{2,1,0:T(8,128)S(1)}, f32[2,384,128]{2,1,0:T(8,128)S(1)}, u32[]{:S(2)}, u32[]{:S(2)}) collective-permute-start(f32[2,384,128]{2,1,0:T(8,128)S(1)} %get-tuple-element.36), channel_id=1, source_target_pairs={{4,8},{8,4},{5,9},{9,5},{6,10},{10,6},{7,11},{11,7},{20,24},{24,20... | collective-permute-start | bytes 1179656 | tf_op jit(solution)/shard_map/ppermute | solution.py:40
  13.0 6.1 %collective-permute-start.4 = (f32[2,2,128,128]{3,2,1,0:T(8,128)S(1)}, f32[2,2,128,128]{3,2,1,0:T(8,128)S(1)}, u32[]{:S(2)}, u32[]{:S(2)}) collective-permute-start(f32[2,2,128,128]{3,2,1,0:T(8,128)S(1)} %pad_maximum_fusion), channel_id=1, source_target_pairs={{0,4},{8,12},{4,0},{12,8},{1,5},{9,13},{5,1},{13,9},{2,6},{10,14},... | collective-permute-start | bytes 786440 | tf_op jit(solution)/shard_map/ppermute | solution.py:40
  15.3 7.9 %collective-permute-start.5 = (f32[2,2,128,128]{3,2,1,0:T(8,128)}, f32[2,2,128,128]{3,2,1,0:T(8,128)S(1)}, u32[]{:S(2)}, u32[]{:S(2)}) collective-permute-start(f32[2,2,128,128]{3,2,1,0:T(8,128)} %pad_maximum_fusion.1), channel_id=1, source_target_pairs={{4,8},{8,4},{5,9},{9,5},{6,10},{10,6},{7,11},{11,7},{20,24},{24,20... | collective-permute-start | bytes 786440 | tf_op jit(solution)/shard_map/ppermute | solution.py:40
  32.5 18.2 %collective-permute-start.6 = (f32[520,256]{1,0:T(8,128)}, f32[520,256]{1,0:T(8,128)S(1)}, u32[]{:S(2)}, u32[]{:S(2)}) collective-permute-start(f32[520,256]{1,0:T(8,128)} %get-tuple-element.20), channel_id=1, source_target_pairs={{0,4},{4,0},{8,12},{12,8},{1,5},{5,1},{9,13},{13,9},{2,6},{6,2},{1... | collective-permute-start | bytes 1597448 | tf_op jit(solution)/shard_map/ppermute | solution.py:45
  32.6 2.5 %collective-permute-start.8 = (f32[2,2,128,128]{3,2,1,0:T(8,128)}, f32[2,2,128,128]{3,2,1,0:T(8,128)S(1)}, u32[]{:S(2)}, u32[]{:S(2)}) collective-permute-start(f32[2,2,128,128]{3,2,1,0:T(8,128)} %get-tuple-element.22), channel_id=1, source_target_pairs={{0,4},{8,12},{4,0},{12,8},{1,5},{9,13},{5,1},{13,9},{2,6},{10,14},... | collective-permute-start | bytes 786440 | tf_op jit(solution)/shard_map/ppermute | solution.py:40
  36.7 23.7 %collective-permute-start.10 = (f32[2,128,512]{2,1,0:T(8,128)}, f32[2,128,512]{2,1,0:T(8,128)}, u32[]{:S(2)}, u32[]{:S(2)}) collective-permute-start(f32[2,128,512]{2,1,0:T(8,128)} %get-tuple-element.46), channel_id=1, source_target_pairs={{1,2},{2,1},{5,6},{6,5},{9,10},{10,9},{13,14},{14,13},{17,18},{18,... | collective-permute-start | bytes 1572872 | tf_op jit(solution)/shard_map/ppermute | solution.py:40
  38.2 24.6 %collective-permute-start.9 = (f32[2,128,512]{2,1,0:T(8,128)S(1)}, f32[2,128,512]{2,1,0:T(8,128)}, u32[]{:S(2)}, u32[]{:S(2)}) collective-permute-start(f32[2,128,512]{2,1,0:T(8,128)S(1)} %get-tuple-element.47), channel_id=1, source_target_pairs={{0,1},{2,3},{1,0},{3,2},{4,5},{6,7},{5,4},{7,6},{8,9},{10,11},{9,8... | collective-permute-start | bytes 1572872 | tf_op jit(solution)/shard_map/ppermute | solution.py:40
  51.9 7.5 %collective-permute-start.7 = (f32[264,256]{1,0:T(8,128)S(1)}, f32[264,256]{1,0:T(8,128)}, u32[]{:S(2)}, u32[]{:S(2)}) collective-permute-start(f32[264,256]{1,0:T(8,128)S(1)} %slice.58), channel_id=1, source_target_pairs={{0,8},{4,12},{8,0},{12,4},{1,9},{5,13},{9,1},{13,5},{2,10},{6,14},... | collective-permute-start | bytes 811016 | tf_op jit(solution)/shard_map/ppermute | solution.py:45
  52.0 8.4 %collective-permute-start.11 = (f32[2,384,128]{2,1,0:T(8,128)S(1)}, f32[2,384,128]{2,1,0:T(8,128)S(1)}, u32[]{:S(2)}, u32[]{:S(2)}) collective-permute-start(f32[2,384,128]{2,1,0:T(8,128)S(1)} %get-tuple-element.24), channel_id=1, source_target_pairs={{0,4},{8,12},{4,0},{12,8},{1,5},{9,13},{5,1},{13,9},{2,6},{10,14},... | collective-permute-start | bytes 1179656 | tf_op jit(solution)/shard_map/ppermute | solution.py:40
  62.8 4.3 %collective-permute-start.12 = (f32[136,256]{1,0:T(8,128)S(1)}, f32[136,256]{1,0:T(8,128)S(1)}, u32[]{:S(2)}, u32[]{:S(2)}) collective-permute-start(f32[136,256]{1,0:T(8,128)S(1)} %slice.49), channel_id=1, source_target_pairs={{0,1},{1,0},{2,3},{3,2},{4,5},{5,4},{6,7},{7,6},{8,9},{9,8},{10,11... | collective-permute-start | bytes 417800 | tf_op jit(solution)/shard_map/ppermute | solution.py:45
  67.1 8.7 %collective-permute-start.13 = (f32[136,256]{1,0:T(8,128)S(1)}, f32[136,256]{1,0:T(8,128)S(1)}, u32[]{:S(2)}, u32[]{:S(2)}) collective-permute-start(f32[136,256]{1,0:T(8,128)S(1)} %maximum_add_fusion.2), channel_id=1, source_target_pairs={{0,2},{1,3},{2,0},{3,1},{4,6},{5,7},{6,4},{7,5},{8,10},{9,11},{10,... | collective-permute-start | bytes 417800 | tf_op jit(solution)/shard_map/ppermute | solution.py:45
  68.6 11.2 %collective-permute-start.15 = (f32[2,384,128]{2,1,0:T(8,128)S(1)}, f32[2,384,128]{2,1,0:T(8,128)S(1)}, u32[]{:S(2)}, u32[]{:S(2)}) collective-permute-start(f32[2,384,128]{2,1,0:T(8,128)S(1)} %maximum_add_fusion), channel_id=1, source_target_pairs={{4,8},{8,4},{5,9},{9,5},{6,10},{10,6},{7,11},{11,7},{20,24},{24,20... | collective-permute-start | bytes 1179656 | tf_op jit(solution)/shard_map/ppermute | solution.py:40
  75.9 6.2 %copy-start = (f32[2,384,384]{2,1,0:T(8,128)S(1)}, f32[2,384,384]{2,1,0:T(8,128)}, u32[]{:S(2)}) copy-start(f32[2,384,384]{2,1,0:T(8,128)} %get-tuple-element.31.inner_ref) | copy-start | bytes 3538948
  75.9 3.9 %collective-permute-start.14 = (f32[128,256]{1,0:T(8,128)S(1)}, f32[128,256]{1,0:T(8,128)S(1)}, u32[]{:S(2)}, u32[]{:S(2)}) collective-permute-start(f32[128,256]{1,0:T(8,128)S(1)} %slice_divide_fusion), channel_id=1, source_target_pairs={{0,1},{1,0},{2,3},{3,2},{4,5},{5,4},{6,7},{7,6},{8,9},{9,8},{10,11... | collective-permute-start | bytes 393224 | tf_op jit(solution)/shard_map/ppermute | solution.py:45
  79.9 5.3 %collective-permute-start.16 = (f32[256,256]{1,0:T(8,128)S(1)}, f32[256,256]{1,0:T(8,128)S(1)}, u32[]{:S(2)}, u32[]{:S(2)}) collective-permute-start(f32[256,256]{1,0:T(8,128)S(1)} %maximum_select_fusion.2), channel_id=1, source_target_pairs={{0,8},{4,12},{8,0},{12,4},{1,9},{5,13},{9,1},{13,5},{2,10},{6,14},... | collective-permute-start | bytes 786440 | tf_op jit(solution)/shard_map/ppermute | solution.py:45
  85.2 5.2 %collective-permute-start.17 = (f32[512,256]{1,0:T(8,128)S(1)}, f32[512,256]{1,0:T(8,128)S(1)}, u32[]{:S(2)}, u32[]{:S(2)}) collective-permute-start(f32[512,256]{1,0:T(8,128)S(1)} %maximum_select_fusion.1), channel_id=1, source_target_pairs={{0,4},{4,0},{8,12},{12,8},{1,5},{5,1},{9,13},{13,9},{2,6},{6,2},{1... | collective-permute-start | bytes 1572872 | tf_op jit(solution)/shard_map/ppermute | solution.py:45

commit v3 on v2

--- a/solution.py
+++ b/solution.py
@@ -141,7 +141,7 @@
         buffers[5][...] = jnp.zeros_like(buffers[5])
     for index in (2, 3):
         windows[index] = jnp.zeros(windows.shape[1:], jnp.float32)
-    for copy in copies:
+    for copy in copies[:-3]:
         copy.wait()
     lane = lax.broadcasted_iota(jnp.int32, (8, LANES), 1)
     sub = lax.broadcasted_iota(jnp.int32, (8, LANES), 0)
@@ -203,13 +203,14 @@
 
         return [functools.partial(some_rows, first) for first in range(0, GROUPS, batch)]
 
-    def right(source, table, target, m):
-        rows = slice(m * W, m * W + W)
+    def right(source, table, target):
         product = jnp.dot(
-            source[rows, :], table[...], preferred_element_type=jnp.float32
+            source[...], table[...], preferred_element_type=jnp.float32
         ).astype(jnp.bfloat16)
-        target[:W, rows] = product[:, :W]
-        target[W:, rows] = product[:, W:]
+        for m in range(MODES):
+            rows = slice(m * W, m * W + W)
+            target[:W, rows] = product[rows, :W]
+            target[W:, rows] = product[rows, W:]
 
     def left(source, table, target, m):
         columns = slice(m * W, m * W + W)
@@ -217,14 +218,14 @@
             table[...], source[:, columns], preferred_element_type=jnp.float32
         )
 
-    def ahead_right(buffers, m):
-        return functools.partial(right, buffers[0], ahead_ref, buffers[1], m)
+    def ahead_right(buffers):
+        return functools.partial(right, buffers[0], ahead_ref, buffers[1])
 
     def ahead_left(buffers, m):
         return functools.partial(left, buffers[1], back_ref, buffers[2], m)
 
-    def back_right(buffers, m):
-        return functools.partial(right, buffers[3], back_ref, buffers[4], m)
+    def back_right(buffers):
+        return functools.partial(right, buffers[3], back_ref, buffers[4])
 
     def back_left(buffers, m):
         return functools.partial(left, buffers[4], ahead_ref, buffers[5], m)
@@ -333,6 +334,8 @@
     x, y = sets
     for each in make_wave(0, x, 0) + make_wave(1, y, 1):
         each()
+    for copy in copies[-3:]:
+        copy.wait()
 
     def pair(index, carry):
         now = (2 * index, 2 * index + 1)
@@ -343,14 +346,14 @@
         adds = add_terms([(past[0], x, other), (past[1], y, other + 1)])
         some = len(adds) * 2 // 3
         merge(
-            [ahead_right(b, m) for b in sets for m in range(MODES)]
+            [ahead_right(b) for b in sets]
             + [ahead_left(x, m) for m in range(MODES)],
             adds[:some],
         )
         merge([ahead_left(y, m) for m in range(MODES)], adds[some:] + weigh(now[0], None, x))
-        merge([back_right(x, m) for m in range(MODES)], weigh(now[1], live, y))
+        merge([back_right(x)], weigh(now[1], live, y))
         merge(
-            [back_right(y, m) for m in range(MODES)]
+            [back_right(y)]
             + [back_left(b, m) for b in sets for m in range(MODES)],
             make_wave(later[0], x, other) + make_wave(later[1], y, other + 1),
         )
@@ -440,8 +443,9 @@
 ):
     row_a, row_b, col_a, col_b = inner_edges(side_ref, inner_ref.shape[1])
     out_ref[...] = inner_ref[...]
-    out_ref[:, row_a, :] += row_a_ref[...]
-    out_ref[:, row_b, :] += row_b_ref[...]
+    tile = inner_ref.shape[1]
+    out_ref[:, row_a, :] += row_a_ref[:, :, :tile]
+    out_ref[:, row_b, :] += row_b_ref[:, :, :tile]
     out_ref[:, :, col_a] += col_a_ref[...]
     out_ref[:, :, col_b] += col_b_ref[...]
 
@@ -510,7 +514,7 @@
         pieces,
     )
 
-    corner = swap(corner, "col", 0)
+    corner, away = barrier((swap(corner, "col", 0), away))
     away = exchange(away, *halvings[0])
     row_a = swap(add_at(row_a, corner[0], (1 - col % 2) * edge), "row", 0)
     row_b = swap(add_at(row_b, corner[1], (1 - col % 2) * edge), "row", 1)
@@ -535,7 +539,7 @@
             part, col_b = barrier((part, col_b))
         elif (axis, bits) != halvings[0]:
             part = gathered(part, axis, bits)
-    result = join(sides, inner, row_a[:, :, :tile], row_b[:, :, :tile], col_a, col_b)
+    result = join(sides, inner, row_a, row_b, col_a, col_b)
     part, result = barrier((part, result))
     whole = gathered(part, *halvings[0])
     return result, whole.reshape(probe.shape)

time: 91.3 us -> 92.6 us (1.014)
  starting transfers between devices: 37 us -> 30.1 us
  Pallas kernels: 11.1 us -> 17 us
  waiting for transfers between devices: 30.7 us -> 33.3 us
  local copies, waits for them, and re-layouts: 4.26 us -> 2.93 us
    ppermute x11, starting transfers between devices: 30.4 us -> 23.3 us  [swap(): return lax.ppermute(x, axis, side_pairs(lax.axis_size(axis), parity))]
    pallas_call x1, Pallas kernels: 9.29 us -> 15.2 us  [slots(): pl.pallas_call(functools.partial(slots_kernel, pieces), out_shape=[jax.Sh...]
    ppermute x7, waiting for transfers between devices: 18.1 us -> 22.5 us  [exchange(): return lax.ppermute(x, axis, [(i, i ^ bits) for i in range(size)])]
    slice x2 -> x0, local copies, waits for them, and re-layouts: 2.05 us -> none  [the longest x1 1.02 us: local(): row_b[:, :, :tile]]
    ppermute x11, waiting for transfers between devices: 12.6 us -> 10.8 us  [swap(): return lax.ppermute(x, axis, side_pairs(lax.axis_size(axis), parity))]
    select_n x3, other arithmetic: 1.12 us -> 2.1 us  [gathered(): jnp.where(first, jnp.concatenate([part, other]), jnp.concatenate([other,...]
    select_n x1, other arithmetic: 0.99 us -> 0.04 us  [local(): jnp.where(row % 2 == 1, first, second)[:, :, tile:]]
  transfers between devices with their start and end apart: 18 -> 18, of which waited for: 10 -> 10; matrix products, arithmetic and copies ran while one was open for 9% -> 7% of each run, Pallas kernels for 2% -> 2%
where the time goes in v3:
time: 92.6 us; the launch traced here: 92.1 us
  waiting for transfers between devices  33.3 us (36%)
  starting transfers between devices  30.1 us (33%)
  Pallas kernels  17 us (18%)
  other arithmetic  7.07 us (8%)
  local copies, waits for them, and re-layouts  2.93 us (3%)
  between operations  1.66 us (2%)
    ppermute x11, starting transfers between devices, swap(): return lax.ppermute(x, axis, side_pairs(lax.axis_size(axis), parity))  23.3 us
    ppermute x7, waiting for transfers between devices, exchange(): return lax.ppermute(x, axis, [(i, i ^ bits) for i in range(size)])  22.5 us
    pallas_call x1, Pallas kernels, slots(): pl.pallas_call(functools.partial(slots_kernel, pieces), out_shape=[jax.Sh...  15.2 us
    ppermute x11, waiting for transfers between devices, swap(): return lax.ppermute(x, axis, side_pairs(lax.axis_size(axis), parity))  10.8 us
    ppermute x7, starting transfers between devices, exchange(): return lax.ppermute(x, axis, [(i, i ^ bits) for i in range(size)])  6.8 us
    select_n x3, other arithmetic, gathered(): jnp.where(first, jnp.concatenate([part, other]), jnp.concatenate([other,...  2.1 us
    dynamic_slice x2, local copies, waits for them, and re-layouts, cut(): return lax.dynamic_slice_in_dim(x, start, HALF, axis=dim)  2.07 us
  transfers between devices with their start and end apart: 18, of which 10 were waited for; matrix products, arithmetic and copies ran while one was open for 7% of the time, Pallas kernels for 2%

profile of v3, /device:TPU:5, one launch (start us, length us, event | category | flops | bytes accessed | tf_op | source)
XLA Modules:
  0.0 92.1 jit_solution(14914926841883774681)
XLA Ops:
  0.6 0.0 copy-start.4
  0.7 2.0 %constant_dynamic-slice_fusion.2 = (f32[2,128,384]{2,1,0:T(8,128)S(1)}, f32[2,128,384]{2,1,0:T(8,128)}) fusion(f32[2,384,384]{2,1,0:T(8,128)} %own_ref.1, s32[]{:T(128)S(6)} %select_n.127, s32[]{:T(128)S(6)} %select_n.126), kind=kLoop, calls=%fused_computation.21 | loop fusion | bytes 1572872 | tf_op jit(solution)/shard_map/dynamic_slice | solution.py:465
  2.7 1.3 %collective-permute-start = (f32[2,128,384]{2,1,0:T(8,128)}, f32[2,128,384]{2,1,0:T(8,128)S(1)}, u32[]{:S(2)}, u32[]{:S(2)}) collective-permute-start(f32[2,128,384]{2,1,0:T(8,128)} %get-tuple-element.43), channel_id=1, source_target_pairs={{0,1},{2,3},{1,0},{3,2},{4,5},{6,7},{5,4},{7,6},{8,9},{10,11},{9,8... | collective-permute-start | bytes 1179656 | tf_op jit(solution)/shard_map/ppermute | solution.py:40
  4.0 0.7 collective-permute-start.1
  4.7 0.1 constant_dynamic-slice_fusion
  4.8 0.0 copy-start.1
  4.8 1.0 %collective-permute-start.2 = (f32[2,384,128]{2,1,0:T(8,128)S(1)}, f32[2,384,128]{2,1,0:T(8,128)S(1)}, u32[]{:S(2)}, u32[]{:S(2)}) collective-permute-start(f32[2,384,128]{2,1,0:T(8,128)S(1)} %get-tuple-element.41), channel_id=1, source_target_pairs={{0,4},{8,12},{4,0},{12,8},{1,5},{9,13},{5,1},{13,9},{2,6},{10,14},... | collective-permute-start | bytes 1179656 | tf_op jit(solution)/shard_map/ppermute | solution.py:40
  5.8 3.0 %collective-permute-start.3 = (f32[2,384,128]{2,1,0:T(8,128)S(1)}, f32[2,384,128]{2,1,0:T(8,128)S(1)}, u32[]{:S(2)}, u32[]{:S(2)}) collective-permute-start(f32[2,384,128]{2,1,0:T(8,128)S(1)} %get-tuple-element.40), channel_id=1, source_target_pairs={{4,8},{8,4},{5,9},{9,5},{6,10},{10,6},{7,11},{11,7},{20,24},{24,20... | collective-permute-start | bytes 1179656 | tf_op jit(solution)/shard_map/ppermute | solution.py:40
  8.8 4.1 %collective-permute-done.row_a_ref = f32[2,128,384]{2,1,0:T(8,128)S(1)} collective-permute-done((f32[2,128,384]{2,1,0:T(8,128)}, f32[2,128,384]{2,1,0:T(8,128)S(1)}, u32[]{:S(2)}, u32[]{:S(2)}) %collective-permute-start) | collective-permute-done | bytes 393248 | tf_op jit(solution)/shard_map/ppermute | solution.py:40
  12.9 0.0 collective-permute-done.1.row_b_ref
  13.0 1.6 %collective-permute-start.4 = (f32[2,2,128,128]{3,2,1,0:T(8,128)S(1)}, f32[2,2,128,128]{3,2,1,0:T(8,128)S(1)}, u32[]{:S(2)}, u32[]{:S(2)}) collective-permute-start(f32[2,2,128,128]{3,2,1,0:T(8,128)S(1)} %pad_maximum_fusion), channel_id=1, source_target_pairs={{0,4},{8,12},{4,0},{12,8},{1,5},{9,13},{5,1},{13,9},{2,6},{10,14},... | collective-permute-start | bytes 786440 | tf_op jit(solution)/shard_map/ppermute | solution.py:40
  14.6 3.0 %collective-permute-start.5 = (f32[2,2,128,128]{3,2,1,0:T(8,128)S(1)}, f32[2,2,128,128]{3,2,1,0:T(8,128)S(1)}, u32[]{:S(2)}, u32[]{:S(2)}) collective-permute-start(f32[2,2,128,128]{3,2,1,0:T(8,128)S(1)} %pad_maximum_fusion.1), channel_id=1, source_target_pairs={{4,8},{8,4},{5,9},{9,5},{6,10},{10,6},{7,11},{11,7},{20,24},{24,20... | collective-permute-start | bytes 786440 | tf_op jit(solution)/shard_map/ppermute | solution.py:40
  18.3 0.1 pad_add_fusion.side_ref
  18.4 0.0 collective-permute-done.2.col_a_ref
  18.4 0.0 collective-permute-done.4.corner_a_ref
  18.4 3.9 %collective-permute-done.5.corner_b_ref = f32[2,2,128,128]{3,2,1,0:T(8,128)S(1)} collective-permute-done((f32[2,2,128,128]{3,2,1,0:T(8,128)S(1)}, f32[2,2,128,128]{3,2,1,0:T(8,128)S(1)}, u32[]{:S(2)}, u32[]{:S(2)}) %collective-permute-start.5) | collective-permute-done | bytes 262176 | tf_op jit(solution)/shard_map/ppermute | solution.py:40
  22.3 15.2 %shard_map.86 = (f32[520,256]{1,0:T(8,128)}, f32[520,256]{1,0:T(8,128)}, f32[2,384,384]{2,1,0:T(8,128)}, f32[2,128,512]{2,1,0:T(8,128)S(1)}, f32[2,128,512]{2,1,...) custom-call(s32[3]{0:T(128)S(1)} %pad_add_fusion.side_ref, ...), custom_call_target="tpu_custom_call" | custom-call | tf_op jit(solution)/shard_map/pallas_call | solution.py:418
  37.5 0.1 collective-permute-start.6
  37.6 1.5 %collective-permute-done.6 = f32[2,2,128,128]{3,2,1,0:T(8,128)S(1)} collective-permute-done((f32[2,2,128,128]{3,2,1,0:T(8,128)S(1)}, f32[2,2,128,128]{3,2,1,0:T(8,128)S(1)}, u32[]{:S(2)}, u32[]{:S(2)}) %collective-permute-start.6) | collective-permute-done | bytes 262176 | tf_op jit(solution)/shard_map/ppermute | solution.py:40
  39.1 0.1 collective-permute-start.7
  39.2 1.6 %fusion = (f32[2,128,512]{2,1,0:T(8,128)}, f32[2,128,512]{2,1,0:T(8,128)S(1)}) fusion(f32[2,128,512]{2,1,0:T(8,128)} %get-tuple-element.27, s32[]{:T(128)S(6)} %select_n.130, f32[2,2,128,128]{3,2,1,0:T(8,128)S(1)} %collective-permute-done.6, f32[2,128,512]{2,1,0:T(8,128)S(1)} %get-tuple-element.25), kind=kLoop, calls=%fused_computation.10 | loop fusion | flops 65536 | bytes 786436 | tf_op jit(solution)/shard_map/dynamic_update_slice | solution.py:470
  40.9 0.7 collective-permute-start.10
  41.6 8.6 %collective-permute-start.9 = (f32[2,128,512]{2,1,0:T(8,128)S(1)}, f32[2,128,512]{2,1,0:T(8,128)S(1)}, u32[]{:S(2)}, u32[]{:S(2)}) collective-permute-start(f32[2,128,512]{2,1,0:T(8,128)S(1)} %get-tuple-element.51), channel_id=1, source_target_pairs={{0,1},{2,3},{1,0},{3,2},{4,5},{6,7},{5,4},{7,6},{8,9},{10,11},{9,8... | collective-permute-start | bytes 1572872 | tf_op jit(solution)/shard_map/ppermute | solution.py:40
  50.2 0.0 collective-permute-done.7
  50.2 1.3 %add.88 = f32[520,256]{1,0:T(8,128)S(1)} add(f32[520,256]{1,0:T(8,128)} %get-tuple-element.21, f32[520,256]{1,0:T(8,128)} %collective-permute-done.7) | non-fusion elementwise | flops 133120 | bytes 1597440 | tf_op jit(solution)/shard_map/add | solution.py:521
  51.5 0.7 slice.50
  52.2 0.0 collective-permute-start.8
  52.2 0.6 collective-permute-start.11
  52.9 7.0 %collective-permute-done.8 = f32[264,256]{1,0:T(8,128)} collective-permute-done((f32[264,256]{1,0:T(8,128)}, f32[264,256]{1,0:T(8,128)}, u32[]{:S(2)}, u32[]{:S(2)}) %collective-permute-start.8) | collective-permute-done | bytes 270368 | tf_op jit(solution)/shard_map/ppermute | solution.py:45
  59.9 1.0 %maximum_add_fusion.1 = f32[264,256]{1,0:T(8,128)S(1)} fusion(f32[264,256]{1,0:T(8,128)} %collective-permute-done.8, f32[8,256]{1,0:T(8,128)S(1)} %slice.49, f32[256,256]{1,0:T(8,128)S(1)} %slice.48), kind=kLoop, calls=%fused_computation.3 | loop fusion | flops 135168 | bytes 811008 | tf_op jit(solution)/shard_map/add | solution.py:525
  60.9 0.0 collective-permute-done.11.col_a_ref
  60.9 1.3 %collective-permute-done.9.row_a_ref = f32[2,128,512]{2,1,0:T(8,128)S(1)} collective-permute-done((f32[2,128,512]{2,1,0:T(8,128)S(1)}, f32[2,128,512]{2,1,0:T(8,128)S(1)}, u32[]{:S(2)}, u32[]{:S(2)}) %collective-permute-start.9) | collective-permute-done | bytes 524320 | tf_op jit(solution)/shard_map/ppermute | solution.py:40
  62.2 1.3 %collective-permute-start.12 = (f32[136,256]{1,0:T(8,128)S(1)}, f32[136,256]{1,0:T(8,128)S(1)}, u32[]{:S(2)}, u32[]{:S(2)}) collective-permute-start(f32[136,256]{1,0:T(8,128)S(1)} %slice.43), channel_id=1, source_target_pairs={{0,1},{1,0},{2,3},{3,2},{4,5},{5,4},{6,7},{7,6},{8,9},{9,8},{10,11... | collective-permute-start | bytes 417800 | tf_op jit(solution)/shard_map/ppermute | solution.py:45
  63.6 3.0 %collective-permute-done.12 = f32[136,256]{1,0:T(8,128)S(1)} collective-permute-done((f32[136,256]{1,0:T(8,128)S(1)}, f32[136,256]{1,0:T(8,128)S(1)}, u32[]{:S(2)}, u32[]{:S(2)}) %collective-permute-start.12) | collective-permute-done | bytes 139296 | tf_op jit(solution)/shard_map/ppermute | solution.py:45
  66.7 0.0 copy-start
  66.7 1.6 %collective-permute-start.13 = (f32[136,256]{1,0:T(8,128)S(1)}, f32[136,256]{1,0:T(8,128)S(1)}, u32[]{:S(2)}, u32[]{:S(2)}) collective-permute-start(f32[136,256]{1,0:T(8,128)S(1)} %maximum_add_fusion.2), channel_id=1, source_target_pairs={{0,2},{1,3},{2,0},{3,1},{4,6},{5,7},{6,4},{7,5},{8,10},{9,11},{10,... | collective-permute-start | bytes 417800 | tf_op jit(solution)/shard_map/ppermute | solution.py:45
  68.3 0.9 maximum_add_fusion
  69.2 2.7 %collective-permute-start.15 = (f32[2,384,128]{2,1,0:T(8,128)}, f32[2,384,128]{2,1,0:T(8,128)S(1)}, u32[]{:S(2)}, u32[]{:S(2)}) collective-permute-start(f32[2,384,128]{2,1,0:T(8,128)} %maximum_add_fusion), channel_id=1, source_target_pairs={{4,8},{8,4},{5,9},{9,5},{6,10},{10,6},{7,11},{11,7},{20,24},{24,20... | collective-permute-start | bytes 1179656 | tf_op jit(solution)/shard_map/ppermute | solution.py:40
  71.9 3.6 %collective-permute-done.13 = f32[136,256]{1,0:T(8,128)S(1)} collective-permute-done((f32[136,256]{1,0:T(8,128)S(1)}, f32[136,256]{1,0:T(8,128)S(1)}, u32[]{:S(2)}, u32[]{:S(2)}) %collective-permute-start.13) | collective-permute-done | bytes 139296 | tf_op jit(solution)/shard_map/ppermute | solution.py:45
  75.6 0.1 collective-permute-start.14
  75.6 3.9 %collective-permute-done.14 = f32[128,256]{1,0:T(8,128)} collective-permute-done((f32[128,256]{1,0:T(8,128)S(1)}, f32[128,256]{1,0:T(8,128)}, u32[]{:S(2)}, u32[]{:S(2)}) %collective-permute-start.14) | collective-permute-done | bytes 131104 | tf_op jit(solution)/shard_map/ppermute | solution.py:45
  79.5 1.0 %maximum_select_fusion.2 = f32[256,256]{1,0:T(8,128)S(1)} fusion(f32[128,256]{1,0:T(8,128)} %collective-permute-done.14, f32[128,256]{1,0:T(8,128)S(1)} %slice_divide_fusion, pred[]{:T(512)S(6)} %eq.35), kind=kLoop, calls=%fused_computation.6 | loop fusion | flops 196608 | bytes 524289 | tf_op jit(solution)/shard_map/jit(_where)/select_n | solution.py:476
  80.6 0.1 collective-permute-start.16
  80.7 1.8 %shard_map.87 = f32[2,384,384]{2,1,0:T(8,128)} custom-call(s32[3]{0:T(128)S(1)} %pad_add_fusion.side_ref, f32[2,384,384]{2,1,0:T(8,128)S(1)} %copy-done, f32[2,128,512]{2,1,0:T(8,128)S(1)} %collective-permute-done.9.row_a_ref, f32[2,128,512]{2,1,0:T(8,128)S(1)} %collective-permute-done.10.row_b_ref, f32[2,384,128]{2,1,0:T(8,128)S(1)} %collective-permute-done.11.col_a_ref, ...), custom_call_target="tpu_custom_call" | custom-call | tf_op jit(solution)/shard_map/pallas_call | solution.py:455
  82.5 3.4 %collective-permute-done.16 = f32[256,256]{1,0:T(8,128)S(1)} collective-permute-done((f32[256,256]{1,0:T(8,128)S(1)}, f32[256,256]{1,0:T(8,128)S(1)}, u32[]{:S(2)}, u32[]{:S(2)}) %collective-permute-start.16) | collective-permute-done | bytes 262176 | tf_op jit(solution)/shard_map/ppermute | solution.py:45
  85.9 3.6 %collective-permute-start.17 = (f32[512,256]{1,0:T(8,128)S(1)}, f32[512,256]{1,0:T(8,128)S(1)}, u32[]{:S(2)}, u32[]{:S(2)}) collective-permute-start(f32[512,256]{1,0:T(8,128)S(1)} %maximum_select_fusion.1), channel_id=1, source_target_pairs={{0,4},{4,0},{8,12},{12,8},{1,5},{5,1},{9,13},{13,9},{2,6},{6,2},{1... | collective-permute-start | bytes 1572872 | tf_op jit(solution)/shard_map/ppermute | solution.py:45
  89.5 1.5 %collective-permute-done.17 = f32[512,256]{1,0:T(8,128)S(1)} collective-permute-done((f32[512,256]{1,0:T(8,128)S(1)}, f32[512,256]{1,0:T(8,128)S(1)}, u32[]{:S(2)}, u32[]{:S(2)}) %collective-permute-start.17) | collective-permute-done | bytes 524320 | tf_op jit(solution)/shard_map/ppermute | solution.py:45
  91.0 1.1 %maximum_select_fusion = f32[1024,256]{1,0:T(8,128)} fusion(f32[512,256]{1,0:T(8,128)S(1)} %collective-permute-done.17, f32[512,256]{1,0:T(8,128)S(1)} %maximum_select_fusion.1, pred[]{:T(512)S(6)} %eq.37), kind=kLoop, calls=%fused_computation | loop fusion | flops 786432 | bytes 2097153 | tf_op jit(solution)/shard_map/jit(_where)/select_n | solution.py:476
  (27 shorter events, 0.3 us)
Async XLA Ops:
  0.6 4.1 %copy-start.4 = (f32[2,384,384]{2,1,0:T(8,128)S(1)}, f32[2,384,384]{2,1,0:T(8,128)}, u32[]{:S(2)}) copy-start(f32[2,384,384]{2,1,0:T(8,128)} %own_ref.1) | copy-start | bytes 3538948
  2.7 10.2 %collective-permute-start = (f32[2,128,384]{2,1,0:T(8,128)}, f32[2,128,384]{2,1,0:T(8,128)S(1)}, u32[]{:S(2)}, u32[]{:S(2)}) collective-permute-start(f32[2,128,384]{2,1,0:T(8,128)} %get-tuple-element.43), channel_id=1, source_target_pairs={{0,1},{2,3},{1,0},{3,2},{4,5},{6,7},{5,4},{7,6},{8,9},{10,11},{9,8... | collective-permute-start | bytes 1179656 | tf_op jit(solution)/shard_map/ppermute | solution.py:40
  4.0 8.9 %collective-permute-start.1 = (f32[2,128,384]{2,1,0:T(8,128)S(1)}, f32[2,128,384]{2,1,0:T(8,128)S(1)}, u32[]{:S(2)}, u32[]{:S(2)}) collective-permute-start(f32[2,128,384]{2,1,0:T(8,128)S(1)} %get-tuple-element.42), channel_id=1, source_target_pairs={{1,2},{2,1},{5,6},{6,5},{9,10},{10,9},{13,14},{14,13},{17,18},{18,... | collective-permute-start | bytes 1179656 | tf_op jit(solution)/shard_map/ppermute | solution.py:40
  4.8 17.5 %copy-start.1 = (s32[1,1,2,8]{3,2,1,0:T(2,128)S(1)}, s32[1,1,2,8]{3,2,1,0:T(2,128)}, u32[]{:S(2)}) copy-start(s32[1,1,2,8]{3,2,1,0:T(2,128)} %param.9) | copy-start | bytes 196
  4.8 13.6 %collective-permute-start.2 = (f32[2,384,128]{2,1,0:T(8,128)S(1)}, f32[2,384,128]{2,1,0:T(8,128)S(1)}, u32[]{:S(2)}, u32[]{:S(2)}) collective-permute-start(f32[2,384,128]{2,1,0:T(8,128)S(1)} %get-tuple-element.41), channel_id=1, source_target_pairs={{0,4},{8,12},{4,0},{12,8},{1,5},{9,13},{5,1},{13,9},{2,6},{10,14},... | collective-permute-start | bytes 1179656 | tf_op jit(solution)/shard_map/ppermute | solution.py:40
  5.8 12.6 %collective-permute-start.3 = (f32[2,384,128]{2,1,0:T(8,128)S(1)}, f32[2,384,128]{2,1,0:T(8,128)S(1)}, u32[]{:S(2)}, u32[]{:S(2)}) collective-permute-start(f32[2,384,128]{2,1,0:T(8,128)S(1)} %get-tuple-element.40), channel_id=1, source_target_pairs={{4,8},{8,4},{5,9},{9,5},{6,10},{10,6},{7,11},{11,7},{20,24},{24,20... | collective-permute-start | bytes 1179656 | tf_op jit(solution)/shard_map/ppermute | solution.py:40
  13.0 5.4 %collective-permute-start.4 = (f32[2,2,128,128]{3,2,1,0:T(8,128)S(1)}, f32[2,2,128,128]{3,2,1,0:T(8,128)S(1)}, u32[]{:S(2)}, u32[]{:S(2)}) collective-permute-start(f32[2,2,128,128]{3,2,1,0:T(8,128)S(1)} %pad_maximum_fusion), channel_id=1, source_target_pairs={{0,4},{8,12},{4,0},{12,8},{1,5},{9,13},{5,1},{13,9},{2,6},{10,14},... | collective-permute-start | bytes 786440 | tf_op jit(solution)/shard_map/ppermute | solution.py:40
  14.6 7.7 %collective-permute-start.5 = (f32[2,2,128,128]{3,2,1,0:T(8,128)S(1)}, f32[2,2,128,128]{3,2,1,0:T(8,128)S(1)}, u32[]{:S(2)}, u32[]{:S(2)}) collective-permute-start(f32[2,2,128,128]{3,2,1,0:T(8,128)S(1)} %pad_maximum_fusion.1), channel_id=1, source_target_pairs={{4,8},{8,4},{5,9},{9,5},{6,10},{10,6},{7,11},{11,7},{20,24},{24,20... | collective-permute-start | bytes 786440 | tf_op jit(solution)/shard_map/ppermute | solution.py:40
  37.5 4.1 %copy-start.2 = (f32[2,384,128]{2,1,0:T(8,128)}, f32[2,384,128]{2,1,0:T(8,128)S(1)}, u32[]{:S(2)}) copy-start(f32[2,384,128]{2,1,0:T(8,128)S(1)} %get-tuple-element.28) | copy-start | bytes 1179652
  37.5 1.6 %collective-permute-start.6 = (f32[2,2,128,128]{3,2,1,0:T(8,128)S(1)}, f32[2,2,128,128]{3,2,1,0:T(8,128)S(1)}, u32[]{:S(2)}, u32[]{:S(2)}) collective-permute-start(f32[2,2,128,128]{3,2,1,0:T(8,128)S(1)} %get-tuple-element.22), channel_id=1, source_target_pairs={{0,4},{8,12},{4,0},{12,8},{1,5},{9,13},{5,1},{13,9},{2,6},{10,14},... | collective-permute-start | bytes 786440 | tf_op jit(solution)/shard_map/ppermute | solution.py:40
  39.1 11.1 %collective-permute-start.7 = (f32[520,256]{1,0:T(8,128)}, f32[520,256]{1,0:T(8,128)}, u32[]{:S(2)}, u32[]{:S(2)}) collective-permute-start(f32[520,256]{1,0:T(8,128)} %get-tuple-element.24), channel_id=1, source_target_pairs={{0,4},{4,0},{8,12},{12,8},{1,5},{5,1},{9,13},{13,9},{2,6},{6,2},{1... | collective-permute-start | bytes 1597448 | tf_op jit(solution)/shard_map/ppermute | solution.py:45
  40.9 20.0 %collective-permute-start.10 = (f32[2,128,512]{2,1,0:T(8,128)}, f32[2,128,512]{2,1,0:T(8,128)S(1)}, u32[]{:S(2)}, u32[]{:S(2)}) collective-permute-start(f32[2,128,512]{2,1,0:T(8,128)} %get-tuple-element.50), channel_id=1, source_target_pairs={{1,2},{2,1},{5,6},{6,5},{9,10},{10,9},{13,14},{14,13},{17,18},{18,... | collective-permute-start | bytes 1572872 | tf_op jit(solution)/shard_map/ppermute | solution.py:40
  41.6 10.6 %copy-start.3 = (f32[2,384,128]{2,1,0:T(8,128)S(1)}, f32[2,384,128]{2,1,0:T(8,128)}, u32[]{:S(2)}) copy-start(f32[2,384,128]{2,1,0:T(8,128)} %copy-done.2) | copy-start | bytes 1179652
  41.6 20.6 %collective-permute-start.9 = (f32[2,128,512]{2,1,0:T(8,128)S(1)}, f32[2,128,512]{2,1,0:T(8,128)S(1)}, u32[]{:S(2)}, u32[]{:S(2)}) collective-permute-start(f32[2,128,512]{2,1,0:T(8,128)S(1)} %get-tuple-element.51), channel_id=1, source_target_pairs={{0,1},{2,3},{1,0},{3,2},{4,5},{6,7},{5,4},{7,6},{8,9},{10,11},{9,8... | collective-permute-start | bytes 1572872 | tf_op jit(solution)/shard_map/ppermute | solution.py:40
  52.2 7.7 %collective-permute-start.8 = (f32[264,256]{1,0:T(8,128)}, f32[264,256]{1,0:T(8,128)}, u32[]{:S(2)}, u32[]{:S(2)}) collective-permute-start(f32[264,256]{1,0:T(8,128)} %slice.50), channel_id=1, source_target_pairs={{0,8},{4,12},{8,0},{12,4},{1,9},{5,13},{9,1},{13,5},{2,10},{6,14},... | collective-permute-start | bytes 811016 | tf_op jit(solution)/shard_map/ppermute | solution.py:45
  52.2 8.7 %collective-permute-start.11 = (f32[2,384,128]{2,1,0:T(8,128)S(1)}, f32[2,384,128]{2,1,0:T(8,128)S(1)}, u32[]{:S(2)}, u32[]{:S(2)}) collective-permute-start(f32[2,384,128]{2,1,0:T(8,128)S(1)} %copy-done.3), channel_id=1, source_target_pairs={{0,4},{8,12},{4,0},{12,8},{1,5},{9,13},{5,1},{13,9},{2,6},{10,14},... | collective-permute-start | bytes 1179656 | tf_op jit(solution)/shard_map/ppermute | solution.py:40
  62.2 4.4 %collective-permute-start.12 = (f32[136,256]{1,0:T(8,128)S(1)}, f32[136,256]{1,0:T(8,128)S(1)}, u32[]{:S(2)}, u32[]{:S(2)}) collective-permute-start(f32[136,256]{1,0:T(8,128)S(1)} %slice.43), channel_id=1, source_target_pairs={{0,1},{1,0},{2,3},{3,2},{4,5},{5,4},{6,7},{7,6},{8,9},{9,8},{10,11... | collective-permute-start | bytes 417800 | tf_op jit(solution)/shard_map/ppermute | solution.py:45
  66.7 14.0 %copy-start = (f32[2,384,384]{2,1,0:T(8,128)S(1)}, f32[2,384,384]{2,1,0:T(8,128)}, u32[]{:S(2)}) copy-start(f32[2,384,384]{2,1,0:T(8,128)} %get-tuple-element.35.inner_ref) | copy-start | bytes 3538948
  66.7 8.8 %collective-permute-start.13 = (f32[136,256]{1,0:T(8,128)S(1)}, f32[136,256]{1,0:T(8,128)S(1)}, u32[]{:S(2)}, u32[]{:S(2)}) collective-permute-start(f32[136,256]{1,0:T(8,128)S(1)} %maximum_add_fusion.2), channel_id=1, source_target_pairs={{0,2},{1,3},{2,0},{3,1},{4,6},{5,7},{6,4},{7,5},{8,10},{9,11},{10,... | collective-permute-start | bytes 417800 | tf_op jit(solution)/shard_map/ppermute | solution.py:45
  69.2 11.4 %collective-permute-start.15 = (f32[2,384,128]{2,1,0:T(8,128)}, f32[2,384,128]{2,1,0:T(8,128)S(1)}, u32[]{:S(2)}, u32[]{:S(2)}) collective-permute-start(f32[2,384,128]{2,1,0:T(8,128)} %maximum_add_fusion), channel_id=1, source_target_pairs={{4,8},{8,4},{5,9},{9,5},{6,10},{10,6},{7,11},{11,7},{20,24},{24,20... | collective-permute-start | bytes 1179656 | tf_op jit(solution)/shard_map/ppermute | solution.py:40
  75.6 4.0 %collective-permute-start.14 = (f32[128,256]{1,0:T(8,128)S(1)}, f32[128,256]{1,0:T(8,128)}, u32[]{:S(2)}, u32[]{:S(2)}) collective-permute-start(f32[128,256]{1,0:T(8,128)S(1)} %slice_divide_fusion), channel_id=1, source_target_pairs={{0,1},{1,0},{2,3},{3,2},{4,5},{5,4},{6,7},{7,6},{8,9},{9,8},{10,11... | collective-permute-start | bytes 393224 | tf_op jit(solution)/shard_map/ppermute | solution.py:45
  80.6 5.3 %collective-permute-start.16 = (f32[256,256]{1,0:T(8,128)S(1)}, f32[256,256]{1,0:T(8,128)S(1)}, u32[]{:S(2)}, u32[]{:S(2)}) collective-permute-start(f32[256,256]{1,0:T(8,128)S(1)} %maximum_select_fusion.2), channel_id=1, source_target_pairs={{0,8},{4,12},{8,0},{12,4},{1,9},{5,13},{9,1},{13,5},{2,10},{6,14},... | collective-permute-start | bytes 786440 | tf_op jit(solution)/shard_map/ppermute | solution.py:45
  85.9 5.1 %collective-permute-start.17 = (f32[512,256]{1,0:T(8,128)S(1)}, f32[512,256]{1,0:T(8,128)S(1)}, u32[]{:S(2)}, u32[]{:S(2)}) collective-permute-start(f32[512,256]{1,0:T(8,128)S(1)} %maximum_select_fusion.1), channel_id=1, source_target_pairs={{0,4},{4,0},{8,12},{12,8},{1,5},{5,1},{9,13},{13,9},{2,6},{6,2},{1... | collective-permute-start | bytes 1572872 | tf_op jit(solution)/shard_map/ppermute | solution.py:45

commit v4 on v3

--- a/solution.py
+++ b/solution.py
@@ -137,10 +137,6 @@
     )
     grad[...] = jnp.zeros_like(grad)
     probe_grad[...] = jnp.zeros_like(probe_grad)
-    for buffers in sets:
-        buffers[5][...] = jnp.zeros_like(buffers[5])
-    for index in (2, 3):
-        windows[index] = jnp.zeros(windows.shape[1:], jnp.float32)
     for copy in copies[:-3]:
         copy.wait()
     lane = lax.broadcasted_iota(jnp.int32, (8, LANES), 1)
@@ -337,13 +333,13 @@
     for copy in copies[-3:]:
         copy.wait()
 
-    def pair(index, carry):
+    def pair(index, carry, opening=False):
         now = (2 * index, 2 * index + 1)
         past = [jnp.maximum(k - 2, 0) for k in now]
         later = [jnp.minimum(k + 2, KMAX - 1) for k in now]
         other = 2 - lax.rem(index, 2) * 2
         live = (now[1] < count).astype(jnp.float32)
-        adds = add_terms([(past[0], x, other), (past[1], y, other + 1)])
+        adds = [] if opening else add_terms([(past[0], x, other), (past[1], y, other + 1)])
         some = len(adds) * 2 // 3
         merge(
             [ahead_right(b) for b in sets]
@@ -359,7 +355,8 @@
         )
         return carry
 
-    lax.fori_loop(0, pairs, pair, 0)
+    pair(0, 0, opening=True)
+    lax.fori_loop(1, pairs, pair, 0)
     final = pairs - 1
     at = lax.rem(final, 2) * 2
     for each in add_terms([(2 * final, x, at), (2 * final + 1, y, at + 1)]):

time: 92.6 us -> 93.5 us (level)
  the two profiles are of different devices: /device:TPU:5 before, /device:TPU:0 now
where the time goes in v4:
time: 93.5 us; the launch traced here: 93.6 us
  waiting for transfers between devices  35.9 us (38%)
  starting transfers between devices  33 us (35%)
  Pallas kernels  13 us (14%)
  other arithmetic  7.06 us (8%)
  local copies, waits for them, and re-layouts  2.93 us (3%)
  between operations  1.68 us (2%)
    ppermute x7, waiting for transfers between devices, exchange(): return lax.ppermute(x, axis, [(i, i ^ bits) for i in range(size)])  26.9 us
    ppermute x11, starting transfers between devices, swap(): return lax.ppermute(x, axis, side_pairs(lax.axis_size(axis), parity))  17.5 us
    ppermute x7, starting transfers between devices, exchange(): return lax.ppermute(x, axis, [(i, i ^ bits) for i in range(size)])  15.5 us
    pallas_call x1, Pallas kernels, slots(): pl.pallas_call(functools.partial(slots_kernel, pieces), out_shape=[jax.Sh...  11.2 us
    ppermute x11, waiting for transfers between devices, swap(): return lax.ppermute(x, axis, side_pairs(lax.axis_size(axis), parity))  8.98 us
    select_n x3, other arithmetic, gathered(): jnp.where(first, jnp.concatenate([part, other]), jnp.concatenate([other,...  2.1 us
    dynamic_slice x2, local copies, waits for them, and re-layouts, cut(): return lax.dynamic_slice_in_dim(x, start, HALF, axis=dim)  2.07 us
  transfers between devices with their start and end apart: 18, of which 8 were waited for; matrix products, arithmetic and copies ran while one was open for 7% of the time, Pallas kernels for 2%

profile of v4, /device:TPU:0, one launch (start us, length us, event | category | flops | bytes accessed | tf_op | source)
XLA Modules:
  0.0 93.6 jit_solution(11909354173991167930)
XLA Ops:
  0.6 0.0 copy-start.4
  0.7 2.0 %constant_dynamic-slice_fusion.2 = (f32[2,128,384]{2,1,0:T(8,128)S(1)}, f32[2,128,384]{2,1,0:T(8,128)}) fusion(f32[2,384,384]{2,1,0:T(8,128)} %own_ref.1, s32[]{:T(128)S(6)} %select_n.127, s32[]{:T(128)S(6)} %select_n.126), kind=kLoop, calls=%fused_computation.21 | loop fusion | bytes 1572872 | tf_op jit(solution)/shard_map/dynamic_slice | solution.py:462
  2.7 3.0 %collective-permute-start = (f32[2,128,384]{2,1,0:T(8,128)}, f32[2,128,384]{2,1,0:T(8,128)S(1)}, u32[]{:S(2)}, u32[]{:S(2)}) collective-permute-start(f32[2,128,384]{2,1,0:T(8,128)} %get-tuple-element.43), channel_id=1, source_target_pairs={{0,1},{2,3},{1,0},{3,2},{4,5},{6,7},{5,4},{7,6},{8,9},{10,11},{9,8... | collective-permute-start | bytes 1179656 | tf_op jit(solution)/shard_map/ppermute | solution.py:40
  5.7 0.7 collective-permute-start.1
  6.4 0.1 constant_dynamic-slice_fusion
  6.5 0.0 copy-start.1
  6.5 0.1 collective-permute-start.2
  6.6 0.7 collective-permute-start.3
  7.3 7.8 %collective-permute-done.row_a_ref = f32[2,128,384]{2,1,0:T(8,128)S(1)} collective-permute-done((f32[2,128,384]{2,1,0:T(8,128)}, f32[2,128,384]{2,1,0:T(8,128)S(1)}, u32[]{:S(2)}, u32[]{:S(2)}) %collective-permute-start) | collective-permute-done | bytes 393248 | tf_op jit(solution)/shard_map/ppermute | solution.py:40
  15.0 0.0 collective-permute-done.1.row_b_ref
  15.1 0.1 collective-permute-start.4
  15.2 0.7 collective-permute-start.5
  16.6 0.1 pad_add_fusion.side_ref
  16.7 0.0 collective-permute-done.2.col_a_ref
  16.7 0.0 collective-permute-done.3.col_b_ref
  16.7 0.0 collective-permute-done.4.corner_a_ref
  16.7 0.0 collective-permute-done.5.corner_b_ref
  16.7 11.2 %shard_map.86 = (f32[520,256]{1,0:T(8,128)}, f32[520,256]{1,0:T(8,128)}, f32[2,384,384]{2,1,0:T(8,128)}, f32[2,128,512]{2,1,0:T(8,128)S(1)}, f32[2,128,512]{2,1,...) custom-call(s32[3]{0:T(128)S(1)} %pad_add_fusion.side_ref, ...), custom_call_target="tpu_custom_call" | custom-call | tf_op jit(solution)/shard_map/pallas_call | solution.py:415
  28.0 3.4 %collective-permute-start.6 = (f32[2,2,128,128]{3,2,1,0:T(8,128)S(1)}, f32[2,2,128,128]{3,2,1,0:T(8,128)S(1)}, u32[]{:S(2)}, u32[]{:S(2)}) collective-permute-start(f32[2,2,128,128]{3,2,1,0:T(8,128)S(1)} %get-tuple-element.22), channel_id=1, source_target_pairs={{0,4},{8,12},{4,0},{12,8},{1,5},{9,13},{5,1},{13,9},{2,6},{10,14},... | collective-permute-start | bytes 786440 | tf_op jit(solution)/shard_map/ppermute | solution.py:40
  31.4 1.2 %collective-permute-done.6 = f32[2,2,128,128]{3,2,1,0:T(8,128)S(1)} collective-permute-done((f32[2,2,128,128]{3,2,1,0:T(8,128)S(1)}, f32[2,2,128,128]{3,2,1,0:T(8,128)S(1)}, u32[]{:S(2)}, u32[]{:S(2)}) %collective-permute-start.6) | collective-permute-done | bytes 262176 | tf_op jit(solution)/shard_map/ppermute | solution.py:40
  32.6 0.4 collective-permute-start.7
  33.0 1.6 %fusion = (f32[2,128,512]{2,1,0:T(8,128)}, f32[2,128,512]{2,1,0:T(8,128)S(1)}) fusion(f32[2,128,512]{2,1,0:T(8,128)} %get-tuple-element.27, s32[]{:T(128)S(6)} %select_n.130, f32[2,2,128,128]{3,2,1,0:T(8,128)S(1)} %collective-permute-done.6, f32[2,128,512]{2,1,0:T(8,128)S(1)} %get-tuple-element.25), kind=kLoop, calls=%fused_computation.10 | loop fusion | flops 65536 | bytes 786436 | tf_op jit(solution)/shard_map/dynamic_update_slice | solution.py:467
  34.6 0.7 collective-permute-start.10
  35.3 7.5 %collective-permute-start.9 = (f32[2,128,512]{2,1,0:T(8,128)S(1)}, f32[2,128,512]{2,1,0:T(8,128)S(1)}, u32[]{:S(2)}, u32[]{:S(2)}) collective-permute-start(f32[2,128,512]{2,1,0:T(8,128)S(1)} %get-tuple-element.51), channel_id=1, source_target_pairs={{0,1},{2,3},{1,0},{3,2},{4,5},{6,7},{5,4},{7,6},{8,9},{10,11},{9,8... | collective-permute-start | bytes 1572872 | tf_op jit(solution)/shard_map/ppermute | solution.py:40
  42.8 0.0 collective-permute-done.7
  42.8 1.3 %add.88 = f32[520,256]{1,0:T(8,128)S(1)} add(f32[520,256]{1,0:T(8,128)} %get-tuple-element.21, f32[520,256]{1,0:T(8,128)} %collective-permute-done.7) | non-fusion elementwise | flops 133120 | bytes 1597440 | tf_op jit(solution)/shard_map/add | solution.py:518
  44.1 0.7 slice.50
  44.8 11.0 %collective-permute-start.8 = (f32[264,256]{1,0:T(8,128)}, f32[264,256]{1,0:T(8,128)}, u32[]{:S(2)}, u32[]{:S(2)}) collective-permute-start(f32[264,256]{1,0:T(8,128)} %slice.50), channel_id=1, source_target_pairs={{0,8},{4,12},{8,0},{12,4},{1,9},{5,13},{9,1},{13,5},{2,10},{6,14},... | collective-permute-start | bytes 811016 | tf_op jit(solution)/shard_map/ppermute | solution.py:45
  55.9 6.7 %collective-permute-done.8 = f32[264,256]{1,0:T(8,128)} collective-permute-done((f32[264,256]{1,0:T(8,128)}, f32[264,256]{1,0:T(8,128)}, u32[]{:S(2)}, u32[]{:S(2)}) %collective-permute-start.8) | collective-permute-done | bytes 270368 | tf_op jit(solution)/shard_map/ppermute | solution.py:45
  62.6 1.0 %maximum_add_fusion.1 = f32[264,256]{1,0:T(8,128)S(1)} fusion(f32[264,256]{1,0:T(8,128)} %collective-permute-done.8, f32[8,256]{1,0:T(8,128)S(1)} %slice.49, f32[256,256]{1,0:T(8,128)S(1)} %slice.48), kind=kLoop, calls=%fused_computation.3 | loop fusion | flops 135168 | bytes 811008 | tf_op jit(solution)/shard_map/add | solution.py:522
  63.6 0.0 collective-permute-done.10.row_b_ref
  63.6 0.0 collective-permute-done.9.row_a_ref
  63.7 0.4 collective-permute-start.12
  64.1 4.7 %collective-permute-done.12 = f32[136,256]{1,0:T(8,128)S(1)} collective-permute-done((f32[136,256]{1,0:T(8,128)S(1)}, f32[136,256]{1,0:T(8,128)S(1)}, u32[]{:S(2)}, u32[]{:S(2)}) %collective-permute-start.12) | collective-permute-done | bytes 139296 | tf_op jit(solution)/shard_map/ppermute | solution.py:45
  68.8 0.0 copy-start
  68.8 0.5 collective-permute-start.13
  69.3 0.9 maximum_add_fusion
  70.2 0.7 collective-permute-start.15
  70.9 5.6 %collective-permute-done.13 = f32[136,256]{1,0:T(8,128)S(1)} collective-permute-done((f32[136,256]{1,0:T(8,128)S(1)}, f32[136,256]{1,0:T(8,128)S(1)}, u32[]{:S(2)}, u32[]{:S(2)}) %collective-permute-start.13) | collective-permute-done | bytes 139296 | tf_op jit(solution)/shard_map/ppermute | solution.py:45
  76.5 0.1 collective-permute-start.14
  76.6 5.1 %collective-permute-done.14 = f32[128,256]{1,0:T(8,128)} collective-permute-done((f32[128,256]{1,0:T(8,128)S(1)}, f32[128,256]{1,0:T(8,128)}, u32[]{:S(2)}, u32[]{:S(2)}) %collective-permute-start.14) | collective-permute-done | bytes 131104 | tf_op jit(solution)/shard_map/ppermute | solution.py:45
  81.7 1.0 %maximum_select_fusion.2 = f32[256,256]{1,0:T(8,128)S(1)} fusion(f32[128,256]{1,0:T(8,128)} %collective-permute-done.14, f32[128,256]{1,0:T(8,128)S(1)} %slice_divide_fusion, pred[]{:T(512)S(6)} %eq.35), kind=kLoop, calls=%fused_computation.6 | loop fusion | flops 196608 | bytes 524289 | tf_op jit(solution)/shard_map/jit(_where)/select_n | solution.py:473
  82.7 3.1 %collective-permute-start.16 = (f32[256,256]{1,0:T(8,128)S(1)}, f32[256,256]{1,0:T(8,128)S(1)}, u32[]{:S(2)}, u32[]{:S(2)}) collective-permute-start(f32[256,256]{1,0:T(8,128)S(1)} %maximum_select_fusion.2), channel_id=1, source_target_pairs={{0,8},{4,12},{8,0},{12,4},{1,9},{5,13},{9,1},{13,5},{2,10},{6,14},... | collective-permute-start | bytes 786440 | tf_op jit(solution)/shard_map/ppermute | solution.py:45
  85.8 1.8 %shard_map.87 = f32[2,384,384]{2,1,0:T(8,128)} custom-call(s32[3]{0:T(128)S(1)} %pad_add_fusion.side_ref, f32[2,384,384]{2,1,0:T(8,128)S(1)} %copy-done, f32[2,128,512]{2,1,0:T(8,128)S(1)} %collective-permute-done.9.row_a_ref, f32[2,128,512]{2,1,0:T(8,128)S(1)} %collective-permute-done.10.row_b_ref, f32[2,384,128]{2,1,0:T(8,128)S(1)} %collective-permute-done.11.col_a_ref, ...), custom_call_target="tpu_custom_call" | custom-call | tf_op jit(solution)/shard_map/pallas_call | solution.py:452
  87.6 2.9 %collective-permute-done.16 = f32[256,256]{1,0:T(8,128)S(1)} collective-permute-done((f32[256,256]{1,0:T(8,128)S(1)}, f32[256,256]{1,0:T(8,128)S(1)}, u32[]{:S(2)}, u32[]{:S(2)}) %collective-permute-start.16) | collective-permute-done | bytes 262176 | tf_op jit(solution)/shard_map/ppermute | solution.py:45
  90.5 0.1 collective-permute-start.17
  90.6 1.9 %collective-permute-done.17 = f32[512,256]{1,0:T(8,128)S(1)} collective-permute-done((f32[512,256]{1,0:T(8,128)S(1)}, f32[512,256]{1,0:T(8,128)S(1)}, u32[]{:S(2)}, u32[]{:S(2)}) %collective-permute-start.17) | collective-permute-done | bytes 524320 | tf_op jit(solution)/shard_map/ppermute | solution.py:45
  92.5 1.1 %maximum_select_fusion = f32[1024,256]{1,0:T(8,128)} fusion(f32[512,256]{1,0:T(8,128)S(1)} %collective-permute-done.17, f32[512,256]{1,0:T(8,128)S(1)} %maximum_select_fusion.1, pred[]{:T(512)S(6)} %eq.37), kind=kLoop, calls=%fused_computation | loop fusion | flops 786432 | bytes 2097153 | tf_op jit(solution)/shard_map/jit(_where)/select_n | solution.py:473
  (27 shorter events, 0.3 us)
Async XLA Ops:
  0.6 5.8 %copy-start.4 = (f32[2,384,384]{2,1,0:T(8,128)S(1)}, f32[2,384,384]{2,1,0:T(8,128)}, u32[]{:S(2)}) copy-start(f32[2,384,384]{2,1,0:T(8,128)} %own_ref.1) | copy-start | bytes 3538948
  2.7 12.3 %collective-permute-start = (f32[2,128,384]{2,1,0:T(8,128)}, f32[2,128,384]{2,1,0:T(8,128)S(1)}, u32[]{:S(2)}, u32[]{:S(2)}) collective-permute-start(f32[2,128,384]{2,1,0:T(8,128)} %get-tuple-element.43), channel_id=1, source_target_pairs={{0,1},{2,3},{1,0},{3,2},{4,5},{6,7},{5,4},{7,6},{8,9},{10,11},{9,8... | collective-permute-start | bytes 1179656 | tf_op jit(solution)/shard_map/ppermute | solution.py:40
  5.7 9.3 %collective-permute-start.1 = (f32[2,128,384]{2,1,0:T(8,128)S(1)}, f32[2,128,384]{2,1,0:T(8,128)S(1)}, u32[]{:S(2)}, u32[]{:S(2)}) collective-permute-start(f32[2,128,384]{2,1,0:T(8,128)S(1)} %get-tuple-element.42), channel_id=1, source_target_pairs={{1,2},{2,1},{5,6},{6,5},{9,10},{10,9},{13,14},{14,13},{17,18},{18,... | collective-permute-start | bytes 1179656 | tf_op jit(solution)/shard_map/ppermute | solution.py:40
  6.5 10.2 %copy-start.1 = (s32[1,1,2,8]{3,2,1,0:T(2,128)S(1)}, s32[1,1,2,8]{3,2,1,0:T(2,128)}, u32[]{:S(2)}) copy-start(s32[1,1,2,8]{3,2,1,0:T(2,128)} %param.9) | copy-start | bytes 196
  6.5 10.2 %collective-permute-start.2 = (f32[2,384,128]{2,1,0:T(8,128)S(1)}, f32[2,384,128]{2,1,0:T(8,128)S(1)}, u32[]{:S(2)}, u32[]{:S(2)}) collective-permute-start(f32[2,384,128]{2,1,0:T(8,128)S(1)} %get-tuple-element.41), channel_id=1, source_target_pairs={{0,4},{8,12},{4,0},{12,8},{1,5},{9,13},{5,1},{13,9},{2,6},{10,14},... | collective-permute-start | bytes 1179656 | tf_op jit(solution)/shard_map/ppermute | solution.py:40
  6.6 10.1 %collective-permute-start.3 = (f32[2,384,128]{2,1,0:T(8,128)S(1)}, f32[2,384,128]{2,1,0:T(8,128)S(1)}, u32[]{:S(2)}, u32[]{:S(2)}) collective-permute-start(f32[2,384,128]{2,1,0:T(8,128)S(1)} %get-tuple-element.40), channel_id=1, source_target_pairs={{4,8},{8,4},{5,9},{9,5},{6,10},{10,6},{7,11},{11,7},{20,24},{24,20... | collective-permute-start | bytes 1179656 | tf_op jit(solution)/shard_map/ppermute | solution.py:40
  15.1 1.6 %collective-permute-start.4 = (f32[2,2,128,128]{3,2,1,0:T(8,128)S(1)}, f32[2,2,128,128]{3,2,1,0:T(8,128)S(1)}, u32[]{:S(2)}, u32[]{:S(2)}) collective-permute-start(f32[2,2,128,128]{3,2,1,0:T(8,128)S(1)} %pad_maximum_fusion), channel_id=1, source_target_pairs={{0,4},{8,12},{4,0},{12,8},{1,5},{9,13},{5,1},{13,9},{2,6},{10,14},... | collective-permute-start | bytes 786440 | tf_op jit(solution)/shard_map/ppermute | solution.py:40
  15.2 1.5 %collective-permute-start.5 = (f32[2,2,128,128]{3,2,1,0:T(8,128)S(1)}, f32[2,2,128,128]{3,2,1,0:T(8,128)S(1)}, u32[]{:S(2)}, u32[]{:S(2)}) collective-permute-start(f32[2,2,128,128]{3,2,1,0:T(8,128)S(1)} %pad_maximum_fusion.1), channel_id=1, source_target_pairs={{4,8},{8,4},{5,9},{9,5},{6,10},{10,6},{7,11},{11,7},{20,24},{24,20... | collective-permute-start | bytes 786440 | tf_op jit(solution)/shard_map/ppermute | solution.py:40
  28.0 7.3 %copy-start.2 = (f32[2,384,128]{2,1,0:T(8,128)}, f32[2,384,128]{2,1,0:T(8,128)S(1)}, u32[]{:S(2)}) copy-start(f32[2,384,128]{2,1,0:T(8,128)S(1)} %get-tuple-element.28) | copy-start | bytes 1179652
  28.0 4.6 %collective-permute-start.6 = (f32[2,2,128,128]{3,2,1,0:T(8,128)S(1)}, f32[2,2,128,128]{3,2,1,0:T(8,128)S(1)}, u32[]{:S(2)}, u32[]{:S(2)}) collective-permute-start(f32[2,2,128,128]{3,2,1,0:T(8,128)S(1)} %get-tuple-element.22), channel_id=1, source_target_pairs={{0,4},{8,12},{4,0},{12,8},{1,5},{9,13},{5,1},{13,9},{2,6},{10,14},... | collective-permute-start | bytes 786440 | tf_op jit(solution)/shard_map/ppermute | solution.py:40
  32.6 10.2 %collective-permute-start.7 = (f32[520,256]{1,0:T(8,128)}, f32[520,256]{1,0:T(8,128)}, u32[]{:S(2)}, u32[]{:S(2)}) collective-permute-start(f32[520,256]{1,0:T(8,128)} %get-tuple-element.24), channel_id=1, source_target_pairs={{0,4},{4,0},{8,12},{12,8},{1,5},{5,1},{9,13},{13,9},{2,6},{6,2},{1... | collective-permute-start | bytes 1597448 | tf_op jit(solution)/shard_map/ppermute | solution.py:45
  34.6 29.0 %collective-permute-start.10 = (f32[2,128,512]{2,1,0:T(8,128)}, f32[2,128,512]{2,1,0:T(8,128)S(1)}, u32[]{:S(2)}, u32[]{:S(2)}) collective-permute-start(f32[2,128,512]{2,1,0:T(8,128)} %get-tuple-element.50), channel_id=1, source_target_pairs={{1,2},{2,1},{5,6},{6,5},{9,10},{10,9},{13,14},{14,13},{17,18},{18,... | collective-permute-start | bytes 1572872 | tf_op jit(solution)/shard_map/ppermute | solution.py:40
  35.3 20.6 %copy-start.3 = (f32[2,384,128]{2,1,0:T(8,128)S(1)}, f32[2,384,128]{2,1,0:T(8,128)}, u32[]{:S(2)}) copy-start(f32[2,384,128]{2,1,0:T(8,128)} %copy-done.2) | copy-start | bytes 1179652
  35.3 28.3 %collective-permute-start.9 = (f32[2,128,512]{2,1,0:T(8,128)S(1)}, f32[2,128,512]{2,1,0:T(8,128)S(1)}, u32[]{:S(2)}, u32[]{:S(2)}) collective-permute-start(f32[2,128,512]{2,1,0:T(8,128)S(1)} %get-tuple-element.51), channel_id=1, source_target_pairs={{0,1},{2,3},{1,0},{3,2},{4,5},{6,7},{5,4},{7,6},{8,9},{10,11},{9,8... | collective-permute-start | bytes 1572872 | tf_op jit(solution)/shard_map/ppermute | solution.py:40
  44.8 17.8 %collective-permute-start.8 = (f32[264,256]{1,0:T(8,128)}, f32[264,256]{1,0:T(8,128)}, u32[]{:S(2)}, u32[]{:S(2)}) collective-permute-start(f32[264,256]{1,0:T(8,128)} %slice.50), channel_id=1, source_target_pairs={{0,8},{4,12},{8,0},{12,4},{1,9},{5,13},{9,1},{13,5},{2,10},{6,14},... | collective-permute-start | bytes 811016 | tf_op jit(solution)/shard_map/ppermute | solution.py:45
  55.9 7.8 %collective-permute-start.11 = (f32[2,384,128]{2,1,0:T(8,128)S(1)}, f32[2,384,128]{2,1,0:T(8,128)S(1)}, u32[]{:S(2)}, u32[]{:S(2)}) collective-permute-start(f32[2,384,128]{2,1,0:T(8,128)S(1)} %copy-done.3), channel_id=1, source_target_pairs={{0,4},{8,12},{4,0},{12,8},{1,5},{9,13},{5,1},{13,9},{2,6},{10,14},... | collective-permute-start | bytes 1179656 | tf_op jit(solution)/shard_map/ppermute | solution.py:40
  63.7 5.1 %collective-permute-start.12 = (f32[136,256]{1,0:T(8,128)S(1)}, f32[136,256]{1,0:T(8,128)S(1)}, u32[]{:S(2)}, u32[]{:S(2)}) collective-permute-start(f32[136,256]{1,0:T(8,128)S(1)} %slice.43), channel_id=1, source_target_pairs={{0,1},{1,0},{2,3},{3,2},{4,5},{5,4},{6,7},{7,6},{8,9},{9,8},{10,11... | collective-permute-start | bytes 417800 | tf_op jit(solution)/shard_map/ppermute | solution.py:45
  68.8 16.9 %copy-start = (f32[2,384,384]{2,1,0:T(8,128)S(1)}, f32[2,384,384]{2,1,0:T(8,128)}, u32[]{:S(2)}) copy-start(f32[2,384,384]{2,1,0:T(8,128)} %get-tuple-element.35.inner_ref) | copy-start | bytes 3538948
  68.8 7.6 %collective-permute-start.13 = (f32[136,256]{1,0:T(8,128)S(1)}, f32[136,256]{1,0:T(8,128)S(1)}, u32[]{:S(2)}, u32[]{:S(2)}) collective-permute-start(f32[136,256]{1,0:T(8,128)S(1)} %maximum_add_fusion.2), channel_id=1, source_target_pairs={{0,2},{1,3},{2,0},{3,1},{4,6},{5,7},{6,4},{7,5},{8,10},{9,11},{10,... | collective-permute-start | bytes 417800 | tf_op jit(solution)/shard_map/ppermute | solution.py:45
  70.2 12.5 %collective-permute-start.15 = (f32[2,384,128]{2,1,0:T(8,128)}, f32[2,384,128]{2,1,0:T(8,128)S(1)}, u32[]{:S(2)}, u32[]{:S(2)}) collective-permute-start(f32[2,384,128]{2,1,0:T(8,128)} %maximum_add_fusion), channel_id=1, source_target_pairs={{4,8},{8,4},{5,9},{9,5},{6,10},{10,6},{7,11},{11,7},{20,24},{24,20... | collective-permute-start | bytes 1179656 | tf_op jit(solution)/shard_map/ppermute | solution.py:40
  76.5 5.1 %collective-permute-start.14 = (f32[128,256]{1,0:T(8,128)S(1)}, f32[128,256]{1,0:T(8,128)}, u32[]{:S(2)}, u32[]{:S(2)}) collective-permute-start(f32[128,256]{1,0:T(8,128)S(1)} %slice_divide_fusion), channel_id=1, source_target_pairs={{0,1},{1,0},{2,3},{3,2},{4,5},{5,4},{6,7},{7,6},{8,9},{9,8},{10,11... | collective-permute-start | bytes 393224 | tf_op jit(solution)/shard_map/ppermute | solution.py:45
  82.7 7.8 %collective-permute-start.16 = (f32[256,256]{1,0:T(8,128)S(1)}, f32[256,256]{1,0:T(8,128)S(1)}, u32[]{:S(2)}, u32[]{:S(2)}) collective-permute-start(f32[256,256]{1,0:T(8,128)S(1)} %maximum_select_fusion.2), channel_id=1, source_target_pairs={{0,8},{4,12},{8,0},{12,4},{1,9},{5,13},{9,1},{13,5},{2,10},{6,14},... | collective-permute-start | bytes 786440 | tf_op jit(solution)/shard_map/ppermute | solution.py:45
  90.5 2.0 %collective-permute-start.17 = (f32[512,256]{1,0:T(8,128)S(1)}, f32[512,256]{1,0:T(8,128)S(1)}, u32[]{:S(2)}, u32[]{:S(2)}) collective-permute-start(f32[512,256]{1,0:T(8,128)S(1)} %maximum_select_fusion.1), channel_id=1, source_target_pairs={{0,4},{4,0},{8,12},{12,8},{1,5},{5,1},{9,13},{13,9},{2,6},{6,2},{1... | collective-permute-start | bytes 1572872 | tf_op jit(solution)/shard_map/ppermute | solution.py:45
